TPU v7x, 32 devices: a whole 2x2x4 slice. The times are simulated.
32 devices in a mesh: ctx: 8 (over y, x, core), exp: 4 (over z).
Axes of the slice: x: 2, y: 2, z: 4, core: 2. Of those that a mesh axis runs over, the one named last changes fastest.
Arguments:
- queries: bfloat16 [4, 1024, 4096], P('exp', 'ctx'), may hold values from -4.5 to 4.5
- keys: bfloat16 [4, 1024, 256], P('exp', 'ctx'), may hold values from -4.5 to 4.5
- values: bfloat16 [4, 1024, 256], P('exp', 'ctx'), may hold values from -12 to 12
- attention_output_grad: bfloat16 [4, 1024, 4096], P('exp', 'ctx'), may hold values from -18 to 18
- span_order: int32 [4, 16], P('exp'), may hold values from 0 to 15, each once within a row
- out_grad: bfloat16 [4, 1024, 4096], P('exp', 'ctx'), may hold values from -6 to 6
- routes: int32 [4, 1024, 2], P('exp', 'ctx'), may hold values from 0 to 15, all different within a row; in each aligned block of 128 rows (0 to 127, 128 to 255, ..., all dimensions but the last counted through in order) at most 24 rows name the same one
- combine: float32 [4, 1024, 2], P('exp', 'ctx'), may hold values from 0.1 to 1
- w_gate: bfloat16 [32, 4096, 768], P(('ctx', 'exp')), may hold values from -0.09375 to 0.09375
- w_up: bfloat16 [32, 4096, 768], P(('ctx', 'exp')), may hold values from -0.09375 to 0.09375
- w_down: bfloat16 [32, 768, 4096], P(('ctx', 'exp')), may hold values from -0.15625 to 0.15625
- gate_up_saved: bfloat16 [32, 32, 24, 1536], P(('ctx', 'exp')), may hold values from -6 to 6
Outputs:
- query_grad: bfloat16 [4, 1024, 4096], P('exp', 'ctx')
- key_grad: bfloat16 [4, 1024, 256], P('exp', 'ctx')
- value_grad: bfloat16 [4, 1024, 256], P('exp', 'ctx')
- token_grad: bfloat16 [4, 1024, 4096], P('exp', 'ctx')
Inputs may be any that keep to these rules, and one draw needn't show every extreme that they name: `routes`: in the rows of one device no expert is named by more than 24 rows.
All inputs are finite; a program needn't handle non-finite values.
Results may differ from a plain program's by a relative error of at most 0.025.
Values may be sent and summed in bfloat16 or wider, within the bound.
No kernel may reach another device: no remote copies, remote signals or barrier semaphores. Data moves between devices by JAX's collectives and lax.ppermute only.
A program may use at most 192 MiB of HBM per device.

v0:
```python
import functools
import math

import jax
import jax.numpy as jnp
from jax import lax
from jax.experimental import pallas as pl
from jax.experimental.pallas import tpu as pltpu
from jax.sharding import PartitionSpec as P

QUERY_HEADS = 32
KEY_VALUE_HEADS = 2
HEAD_SIZE = 128
TOPK = 2
NEG = -1e30
LOG2E = math.log2(math.e)
HEADS_STEP = 8
PARTS = 4
EXTRA = 128
VMEM = 56 * 1024 * 1024


def swap(value, mask):
    count = lax.axis_size("ctx")
    return lax.ppermute(value, "ctx", [(i, i ^ mask) for i in range(count)])


def turn(value, steps=1):
    count = lax.axis_size("exp")
    return lax.ppermute(value, "exp", [(i, (i + steps) % count) for i in range(count)])


def rows_dot(a, b, dims):
    return lax.dot_general(a, b, (dims, ((), ())), preferred_element_type=jnp.float32)


def attention_kernel(
    bias_ref, q_ref, g_ref, k_ref, v_ref, dk_in, dv_in, *refs, after
):
    dq_ref, dk_ref, dv_ref = refs[after:]
    step = pl.program_id(0)
    scale = HEAD_SIZE ** (-0.5)
    heads = q_ref.shape[1] // HEAD_SIZE
    k = k_ref[...]
    v = v_ref[...]
    qs = jnp.concatenate(
        [q_ref[:, h * HEAD_SIZE : (h + 1) * HEAD_SIZE] for h in range(heads)], axis=0
    )
    gs = jnp.concatenate(
        [g_ref[:, h * HEAD_SIZE : (h + 1) * HEAD_SIZE] for h in range(heads)], axis=0
    )
    bias = jnp.concatenate([bias_ref[...]] * heads, axis=1)
    scores = rows_dot(k, qs, ((1,), (1,))) * (scale * LOG2E) + bias
    peak = jnp.max(scores, axis=0, keepdims=True)
    weights = jnp.exp2(scores - peak)
    dprobs = rows_dot(v, gs, ((1,), (1,)))
    total = jnp.sum(weights, axis=0, keepdims=True)
    weighted = jnp.sum(weights * dprobs, axis=0, keepdims=True)
    inverse = 1.0 / total
    delta = weighted * inverse
    probs = weights * inverse
    dscores = (probs * (dprobs - delta) * scale).astype(jnp.bfloat16)
    probs_low = probs.astype(jnp.bfloat16)
    dq = rows_dot(dscores, k, ((0,), (0,)))
    for h in range(heads):
        dq_ref[:, h * HEAD_SIZE : (h + 1) * HEAD_SIZE] = dq[
            h * q_ref.shape[0] : (h + 1) * q_ref.shape[0]
        ].astype(jnp.bfloat16)
    dk = rows_dot(dscores, qs, ((1,), (0,)))
    dv = rows_dot(probs_low, gs, ((1,), (0,)))

    @pl.when(step == 0)
    def _():
        dk_ref[...] = dk_in[...] + dk
        dv_ref[...] = dv_in[...] + dv

    @pl.when(step > 0)
    def _():
        dk_ref[...] += dk
        dv_ref[...] += dv


def attention(part, parts, bias, queries, grads, both, sums, after=()):
    rows = queries.shape[0]
    key_rows = both.shape[0]
    steps = QUERY_HEADS // parts // HEADS_STEP
    group = part * KEY_VALUE_HEADS // parts
    wide = pl.BlockSpec((rows, HEADS_STEP * HEAD_SIZE), lambda i: (0, part * steps + i))
    key_part = pl.BlockSpec((key_rows, HEAD_SIZE), lambda i: (0, group))
    value_part = pl.BlockSpec((key_rows, HEAD_SIZE), lambda i: (0, KEY_VALUE_HEADS + group))
    acc = pl.BlockSpec((key_rows, HEAD_SIZE), lambda i: (0, 0))
    acc_shape = jax.ShapeDtypeStruct((key_rows, HEAD_SIZE), jnp.float32)
    own = pl.BlockSpec((rows, HEADS_STEP * HEAD_SIZE), lambda i: (0, i))
    return pl.pallas_call(
        functools.partial(attention_kernel, after=len(after)),
        grid=(steps,),
        in_specs=[pl.BlockSpec((key_rows, rows), lambda i: (0, 0)), wide, wide]
        + [key_part, value_part, acc, acc]
        + [pl.BlockSpec(memory_space=pl.ANY)] * len(after),
        out_specs=[own, acc, acc],
        out_shape=[
            jax.ShapeDtypeStruct((rows, QUERY_HEADS // parts * HEAD_SIZE), jnp.bfloat16),
            acc_shape,
            acc_shape,
        ],
        compiler_params=pltpu.CompilerParams(vmem_limit_bytes=VMEM),
        name="attention_core",
    )(bias, queries, grads, both, both, *sums, *after)


def pack_kernel(tokens_ref, routes_ref, combine_ref, out_ref):
    rows, width = tokens_ref.shape
    out_ref[:, :width] = tokens_ref[...]
    weights = combine_ref[...]
    high = weights.astype(jnp.bfloat16).astype(jnp.float32)
    names = routes_ref[...].astype(jnp.float32)
    blank = jnp.zeros((EXTRA - 3 * TOPK, rows), jnp.float32)
    flat = jnp.concatenate([names, high, weights - high, blank], axis=0)
    out_ref[:, width:] = flat.T.astype(jnp.bfloat16)


def pack_tokens(tokens, routes, combine):
    rows, width = tokens.shape
    return pl.pallas_call(
        pack_kernel,
        out_shape=jax.ShapeDtypeStruct((rows, width + EXTRA), jnp.bfloat16),
        compiler_params=pltpu.CompilerParams(vmem_limit_bytes=VMEM),
        name="pack_tokens",
    )(tokens, routes.T, combine.T)


def slot_rows(extra_ref, capacity):
    tall = extra_ref[...].astype(jnp.float32)
    flat = tall.T
    tokens = tall.shape[0]
    t_from = lax.broadcasted_iota(jnp.int32, (tokens, tokens), 0)
    t_to = lax.broadcasted_iota(jnp.int32, (tokens, tokens), 1)
    slots = []
    for k in range(TOPK):
        name = flat[k : k + 1]
        rank = 0.0
        for k_from in range(TOPK):
            same = tall[:, k_from : k_from + 1] == name
            earlier = (t_from * TOPK + k_from) < (t_to * TOPK + k)
            rank = rank + jnp.sum(jnp.where(same & earlier, 1.0, 0.0), axis=0, keepdims=True)
        slots.append(name * capacity + rank)
    weights = [flat[TOPK + k : TOPK + k + 1] + flat[2 * TOPK + k : 2 * TOPK + k + 1] for k in range(TOPK)]
    return slots + weights


def slots_kernel(capacity, after, ids_ref, own_x, other_x, own_ref, other_ref, *refs):
    meta_ref, place_ref, factor_ref = refs[-3:]
    outs = refs[after:-3]

    @pl.when(pl.program_id(0) == 0)
    def _():
        places = []
        factor = 0.0
        for rel, extra in enumerate((own_x, other_x)):
            rows = slot_rows(extra, capacity)
            for index, row in enumerate(rows):
                meta_ref[rel, index : index + 1, :] = row
            ids = ids_ref[:, rel : rel + 1]
            first, second = rows[0] == ids, rows[1] == ids
            places.append(jnp.where(first | second, 1.0, 0.0))
            factor = factor + jnp.sum(
                jnp.where(first, rows[2], 0.0) + jnp.where(second, rows[3], 0.0),
                axis=1,
                keepdims=True,
            )
        place_ref[...] = jnp.concatenate(places, axis=1).astype(jnp.bfloat16)
        factor_ref[...] = factor

    tokens = jnp.concatenate([own_ref[...], other_ref[...]], axis=0)
    rows = rows_dot(place_ref[...], tokens, ((1,), (0,))) * factor_ref[...]
    rows = rows.astype(jnp.bfloat16)
    size = outs[0].shape[0]
    for index, out in enumerate(outs):
        out[...] = rows[index * size : (index + 1) * size]


def build_slots(ids, capacity, own, other, pieces, after=(), blocks=2):
    rows = own.shape[0]
    width = own.shape[1] - EXTRA
    size = ids.shape[0] // pieces
    cols = width // blocks
    part = pl.BlockSpec((rows, cols), lambda i: (0, i))
    extra = pl.BlockSpec((rows, EXTRA), lambda i: (0, width // EXTRA))
    out = pl.pallas_call(
        functools.partial(slots_kernel, capacity, len(after)),
        grid=(blocks,),
        in_specs=[pl.BlockSpec(ids.shape, lambda i: (0, 0)), extra, extra, part, part]
        + [pl.BlockSpec(memory_space=pl.ANY)] * len(after),
        out_specs=[pl.BlockSpec((size, cols), lambda i: (0, i))] * pieces
        + [pl.BlockSpec((2, 2 * TOPK, rows), lambda i: (0, 0, 0))],
        out_shape=[jax.ShapeDtypeStruct((size, width), jnp.bfloat16)] * pieces
        + [jax.ShapeDtypeStruct((2, 2 * TOPK, rows), jnp.float32)],
        scratch_shapes=[
            pltpu.VMEM((ids.shape[0], 2 * rows), jnp.bfloat16),
            pltpu.VMEM((ids.shape[0], 1), jnp.float32),
        ],
        compiler_params=pltpu.CompilerParams(vmem_limit_bytes=VMEM),
        name="build_slots",
    )(ids, own, other, own, other, *after)
    return out[:-1], out[-1]


def tokens_kernel(count, adds, ids_ref, meta_ref, *refs):
    pieces, (own_ref, other_ref) = refs[:count], refs[-2:]
    rows = jnp.concatenate([piece[...] for piece in pieces], axis=0)
    for rel, out in ((1, other_ref), (0, own_ref)):
        ids = ids_ref[:, rel : rel + 1]
        place = (meta_ref[rel, 0:1, :] == ids) | (meta_ref[rel, 1:2, :] == ids)
        place = jnp.where(place, 1.0, 0.0).astype(jnp.bfloat16)
        total = rows_dot(place, rows, ((0,), (0,)))
        if adds and rel == 0:
            total = total + refs[count][...].astype(jnp.float32)
        out[...] = total.astype(out.dtype)


def gather_tokens(ids, meta, pieces, received=(), after=(), blocks=2):
    size, width = pieces[0].shape
    tokens = meta.shape[2]
    cols = width // blocks
    part = pl.BlockSpec((size, cols), lambda i: (0, i))
    whole = pl.BlockSpec((tokens, cols), lambda i: (0, i))
    return pl.pallas_call(
        functools.partial(tokens_kernel, len(pieces), len(received)),
        grid=(blocks,),
        in_specs=[
            pl.BlockSpec(ids.shape, lambda i: (0, 0)),
            pl.BlockSpec(meta.shape, lambda i: (0, 0, 0)),
        ]
        + [part] * len(pieces)
        + [whole] * len(received)
        + [pl.BlockSpec(memory_space=pl.ANY)] * len(after),
        out_specs=[whole, whole],
        out_shape=[
            jax.ShapeDtypeStruct((tokens, width), jnp.float32),
            jax.ShapeDtypeStruct((tokens, width), jnp.bfloat16),
        ],
        compiler_params=pltpu.CompilerParams(vmem_limit_bytes=VMEM),
        name="gather_tokens",
    )(ids, meta, *pieces, *received, *after)


def expert_kernel(count, half, after, saved_ref, down_ref, gate_ref, up_ref, *refs):
    pieces, refs = refs[:count], refs[count + after :]
    outs = refs[:count]
    hidden, gate_low, up_low = refs[count:]
    step = pl.program_id(0)
    width = gate_low.shape[1]
    size = outs[0].shape[0]

    @pl.when(step < half)
    def _():
        rows = jnp.concatenate([piece[...] for piece in pieces], axis=0)
        product = rows_dot(rows, down_ref[...], ((1,), (1,)))

        @pl.when(step == 0)
        def _():
            hidden[...] = product

        @pl.when(step > 0)
        def _():
            hidden[...] += product

    @pl.when(step == half)
    def _():
        total = hidden[...]
        gate = saved_ref[:, :width].astype(jnp.float32)
        up = saved_ref[:, width:].astype(jnp.float32)
        sig = 1.0 / (1.0 + jnp.exp(-gate))
        gate_low[...] = (total * up * sig * (1.0 + gate * (1.0 - sig))).astype(jnp.bfloat16)
        up_low[...] = (total * gate * sig).astype(jnp.bfloat16)

    @pl.when(step >= half)
    def _():
        result = rows_dot(gate_low[...], gate_ref[...], ((1,), (1,)))
        result = (result + rows_dot(up_low[...], up_ref[...], ((1,), (1,)))).astype(jnp.bfloat16)
        for index, out in enumerate(outs):
            out[...] = result[index * size : (index + 1) * size]


def expert(saved, w_down, w_gate, w_up, pieces, after=(), half=2):
    size, width = pieces[0].shape
    hidden = w_down.shape[0]
    count = len(pieces)
    cols = width // half
    early = lambda i: (0, jnp.minimum(i, half - 1))
    late = lambda i: (jnp.maximum(i - half, 0), 0)
    rows = size * count
    return pl.pallas_call(
        functools.partial(expert_kernel, count, half, len(after)),
        grid=(2 * half,),
        in_specs=[
            pl.BlockSpec((rows, 2 * hidden), lambda i: (0, 0)),
            pl.BlockSpec((hidden, cols), early),
            pl.BlockSpec((cols, hidden), late),
            pl.BlockSpec((cols, hidden), late),
        ]
        + [pl.BlockSpec((size, cols), early)] * count
        + [pl.BlockSpec(memory_space=pl.ANY)] * len(after),
        out_specs=[pl.BlockSpec((size, cols), lambda i: (0, jnp.maximum(i - half, 0)))] * count,
        out_shape=[jax.ShapeDtypeStruct((size, width), jnp.bfloat16)] * count,
        scratch_shapes=[
            pltpu.VMEM((rows, hidden), jnp.float32),
            pltpu.VMEM((rows, hidden), jnp.bfloat16),
            pltpu.VMEM((rows, hidden), jnp.bfloat16),
        ],
        compiler_params=pltpu.CompilerParams(vmem_limit_bytes=VMEM),
        name="expert_piece",
    )(saved, w_down, w_gate, w_up, *pieces, *after)


def positions(span_ids, row_ids, span):
    slots = jnp.arange(span_ids.shape[0], dtype=jnp.int32)
    found = jnp.sum(
        jnp.where((row_ids // span)[:, None] == slots[None, :], span_ids[None, :], 0), axis=1
    )
    return found * span + row_ids % span


def shards(
    queries,
    keys,
    values,
    attention_output_grad,
    span_order,
    out_grad,
    routes,
    combine,
    w_gate,
    w_up,
    w_down,
    gate_up_saved,
):
    ctx_size = lax.axis_size("ctx")
    exp_size = lax.axis_size("exp")
    ctx_index = lax.axis_index("ctx")
    exp_index = lax.axis_index("exp")
    tokens = queries.shape[1]
    span = tokens // 2
    chips = ctx_size // 2

    capacity = gate_up_saved.shape[2]
    packed = pack_tokens(out_grad[0], routes[0], combine[0])

    both = jnp.concatenate([keys[0], values[0]], axis=1)
    width_kv = keys.shape[2]
    gathered = lax.all_to_all(
        jnp.broadcast_to(both[None], (ctx_size, *both.shape)), "ctx", 0, 0, tiled=True
    )
    gathered = gathered.reshape(ctx_size * tokens, 2 * width_kv)
    row = jnp.arange(ctx_size * tokens, dtype=jnp.int32)
    key_pos = positions(span_order[0], row, span)
    query_pos = positions(
        span_order[0], ctx_index * tokens + jnp.arange(tokens, dtype=jnp.int32), span
    )
    bias = jnp.where(key_pos[:, None] <= query_pos[None, :], 0.0, NEG).astype(jnp.float32)

    padded = -(-capacity // 8) * 8
    m_ids = jnp.arange(chips, dtype=jnp.int32)
    owner = ((ctx_index ^ (2 * m_ids)) * exp_size + exp_index) // 2
    j_ids = jnp.arange(padded, dtype=jnp.int32)
    slot_ids = jnp.where(j_ids < capacity, owner[:, None] * capacity + j_ids, -1)
    rel = jnp.arange(2, dtype=jnp.int32)
    ids = jnp.where(
        rel[None, :, None, None] == rel[None, None, None, :], slot_ids[:, None, :, None], -1
    )
    ids = ids.reshape(chips * 2 * padded, 2).astype(jnp.float32)

    saved = gate_up_saved[0]
    if padded != capacity:
        saved = jnp.pad(saved, ((0, 0), (0, padded - capacity), (0, 0)))
    j_ctx = ctx_index ^ jnp.arange(ctx_size, dtype=jnp.int32)
    s_exp = (exp_index - jnp.arange(exp_size, dtype=jnp.int32)) % exp_size
    picks = (j_ctx[None, :] * exp_size + s_exp[:, None]).reshape(-1)
    saved = jnp.take(saved, picks, axis=0, mode="clip")
    saved = saved.reshape(exp_size, ctx_size * padded, saved.shape[2])

    def across(pieces, gate=()):
        if gate:
            pieces = lax.optimization_barrier((*pieces, *gate))[: len(pieces)]
        return [pieces[0]] + [swap(piece, 2 * m) for m, piece in enumerate(pieces) if m > 0]

    held = [packed]
    other = [swap(packed, 1)]
    last = ()
    slots, sent, rows, results, metas = {}, {}, {}, {}, {}
    attention_parts = []
    zero = jnp.zeros((ctx_size * tokens, HEAD_SIZE), jnp.float32)
    coming = [turn(packed)]

    def arrive(needs=()):
        nonlocal last
        got, *last = lax.optimization_barrier((coming[-1], *last, *needs))
        last = tuple(last[:1])
        held.append(got)
        other.append(swap(got, 1))
        if len(held) < exp_size:
            coming.append(turn(got))

    def build(s, needs=()):
        nonlocal last
        slots[s], metas[s] = build_slots(ids, capacity, held[s], other[s], chips, (*last, *needs))
        last = (slots[s][0],)

    def apply(s, needs=()):
        nonlocal last
        rows[s] = expert(saved[s], w_down[0], w_gate[0], w_up[0], sent[s], (*last, *needs))
        last = (rows[s][0],)

    def gather(s, received=(), needs=()):
        nonlocal last
        own, sibling = gather_tokens(ids, metas[s], results[s], received, (*last, *needs))
        total = own + swap(sibling, 1).astype(jnp.float32)
        total = total.astype(jnp.bfloat16)
        last = (total,)
        return total

    def attend(part, needs=()):
        nonlocal last
        first = part % (PARTS // KEY_VALUE_HEADS) == 0
        sums = (zero, zero) if first else attention_parts[-1][1:]
        done = attention(
            part,
            PARTS,
            bias,
            queries[0],
            attention_output_grad[0],
            gathered,
            sums,
            (*last, *needs),
        )
        last = (done[0],)
        attention_parts.append(done)

    def send(s, gate=()):
        sent[s] = across(slots[s], gate)

    def back(s, gate=()):
        results[s] = across(rows[s], gate)

    build(0)
    send(0)
    attend(0)
    arrive(sent[0][1:])
    attend(1)
    build(1)
    send(1)
    apply(0)
    arrive(sent[1][1:])
    build(2)
    send(2)
    apply(1)
    ring = ()
    for s in range(3, exp_size):
        arrive(sent[s - 1][1:])
        back(s - 2, sent[s - 1][1:])
        if s == 3:
            attend(2)
        build(s)
        if s == 3:
            attend(3)
        send(s, results[s - 2][1:])
        total = gather(s - 2, ring)
        ring = (turn(total),)
        apply(s - 1)
        if s == exp_size - 1:
            back(s - 1, sent[s][1:])
    apply(exp_size - 1, sent[exp_size - 1][1:])
    back(exp_size - 1, results[exp_size - 2][1:])
    ring = (turn(gather(exp_size - 2, ring)),)
    back(0, results[exp_size - 1][1:])
    ring = (turn(gather(exp_size - 1, ring)),)
    token_out = gather(0, ring)[None]

    query_out = jnp.concatenate([done[0] for done in attention_parts], axis=1)
    ends = attention_parts[PARTS // KEY_VALUE_HEADS - 1 :: PARTS // KEY_VALUE_HEADS]
    key_part = jnp.concatenate([done[1] for done in ends], axis=1).astype(jnp.bfloat16)
    value_part = jnp.concatenate([done[2] for done in ends], axis=1).astype(jnp.bfloat16)
    part = jnp.concatenate([key_part, value_part], axis=1)
    part = part.reshape(ctx_size, tokens, 2 * width_kv)
    part = lax.all_to_all(part, "ctx", 0, 0, tiled=True).astype(jnp.float32)
    part = jnp.sum(part, axis=0, keepdims=True).astype(jnp.bfloat16)
    return (query_out[None], part[..., :width_kv], part[..., width_kv:], token_out)


def solution(mesh):
    row = P("exp", "ctx", None)
    piece = P(("ctx", "exp"), None, None)
    in_specs = (row, row, row, row, P("exp", None), row, row, row) + (piece,) * 3 + (
        P(("ctx", "exp"), None, None, None),
    )
    return jax.shard_map(
        shards, mesh=mesh, in_specs=in_specs, out_specs=(row,) * 4, check_vma=False
    )
```

profile of v0, /device:TPU:0, one launch (start us, length us, event | category | flops | bytes accessed | tf_op | source)
XLA Modules:
  0.0 261.3 jit_solution(10747129915597416855)
XLA Ops:
  0.7 2.5 pack_tokens.1.own_x.own_ref
  3.2 3.0 %collective-permute-start.1 = (bf16[128,4224]{1,0:T(8,128)(2,1)}, bf16[128,4224]{1,0:T(8,128)(2,1)}, u32[]{:S(2)}, u32[]{:S(2)}) collective-permute-start(bf16[128,4224]{1,0:T(8,128)(2,1)} %pack_tokens.1.own_x.own_ref), channel_id=1, source_target_pairs={{0,1},{1,2},{2,3},{3,0},{4,5},{5,6},{6,7},{7,4},{8,9},{9,10},{10,1... | collective-permute-start | bytes 3244040 | tf_op jit(solution)/shard_map/ppermute | solution.py:30
  7.3 3.8 %all-to-all-start = ((bf16[8,128,512]{2,1,0:T(8,128)(2,1)}), bf16[8,128,512]{2,1,0:T(8,128)(2,1)S(1)}, u32[]{:S(2)}, u32[]{:S(2)}) async-start(bf16[8,128,512]{2,1,0:T(8,128)(2,1)} %broadcast_in_dim.104), calls=%async_computation | async-start | bytes 2097152 | tf_op jit(solution)/shard_map/all_to_all | solution.py:351
  12.3 3.3 %build_slots.4 = (bf16[48,4096]{1,0:T(8,128)(2,1)}, bf16[48,4096]{1,0:T(8,128)(2,1)}, bf16[48,4096]{1,0:T(8,128)(2,1)}, bf16[48,4096]{1,0:T(8,128)(2,1)}, f32[2,4,128]{2,1,0:T(4,128)}) custom-call(f32[192,2]{1,0:T(8,128)} %select_convert_fusion.ids_ref, bf16[128,4224]{1,0:T(8,128)(2,1)} %pack_tokens.1.own_x.own_ref, ...), custom_call_target="tpu_custom_call" | custom-call | tf_op jit(solution)/shard_map/build_slots/pallas_call | solution.py:189
  15.6 2.0 collective-permute-start.2
  20.2 6.9 %all-to-all-done = bf16[8,128,512]{2,1,0:T(8,128)(2,1)S(1)} async-done(((bf16[8,128,512]{2,1,0:T(8,128)(2,1)}), bf16[8,128,512]{2,1,0:T(8,128)(2,1)S(1)}, u32[]{:S(2)}, u32[]{:S(2)}) %all-to-all-start) | async-done | bytes 1048608 | tf_op jit(solution)/shard_map/all_to_all | solution.py:351
  28.2 6.4 %attention_core.4 = (bf16[128,1024]{1,0:T(8,128)(2,1)}, f32[1024,128]{1,0:T(8,128)}, f32[1024,128]{1,0:T(8,128)}) custom-call(f32[1024,128]{1,0:T(8,128)} %compare_select_fusion.bias_ref, bf16[128,4096]{1,0:T(8,128)(2,1)} %bitcast.53, bf16[128,4096]{1,0:T(8,128)(2,1)} %bitcast.57, bf16[1024,512]{1,0:T(8,128)(2,1)} %bitcast.45, bf16[1024,512]{1,0:T(8,128)(2,1)} %bitcast.46, ...), custom_call_target="tpu_custom_call" | custom-call | tf_op jit(solution)/shard_map/attention_core/pallas_call | solution.py:94
  34.7 8.9 %collective-permute-done.4.refs_3_ = bf16[48,4096]{1,0:T(8,128)(2,1)} collective-permute-done((bf16[48,4096]{1,0:T(8,128)(2,1)}, bf16[48,4096]{1,0:T(8,128)(2,1)}, u32[]{:S(2)}, u32[]{:S(2)}) %collective-permute-start.4) | collective-permute-done | bytes 393248 | tf_op jit(solution)/shard_map/ppermute | solution.py:25
  43.5 2.1 collective-permute-start.5
  45.8 2.2 gather_fusion
  48.0 6.4 %attention_core.5 = (bf16[128,1024]{1,0:T(8,128)(2,1)}, f32[1024,128]{1,0:T(8,128)}, f32[1024,128]{1,0:T(8,128)}) custom-call(f32[1024,128]{1,0:T(8,128)} %compare_select_fusion.bias_ref, bf16[128,4096]{1,0:T(8,128)(2,1)} %bitcast.54, bf16[128,4096]{1,0:T(8,128)(2,1)} %bitcast.58, bf16[1024,512]{1,0:T(8,128)(2,1)} %bitcast.47, bf16[1024,512]{1,0:T(8,128)(2,1)} %bitcast.48, ...), custom_call_target="tpu_custom_call" | custom-call | tf_op jit(solution)/shard_map/attention_core/pallas_call | solution.py:94
  54.4 3.5 %build_slots.5 = (bf16[48,4096]{1,0:T(8,128)(2,1)}, bf16[48,4096]{1,0:T(8,128)(2,1)}, bf16[48,4096]{1,0:T(8,128)(2,1)}, bf16[48,4096]{1,0:T(8,128)(2,1)}, f32[2,4,128]{2,1,0:T(4,128)}) custom-call(f32[192,2]{1,0:T(8,128)} %select_convert_fusion.ids_ref, bf16[128,4224]{1,0:T(8,128)(2,1)} %collective-permute-done.1.own_x.own_ref, ...), custom_call_target="tpu_custom_call" | custom-call | tf_op jit(solution)/shard_map/build_slots/pallas_call | solution.py:189
  58.8 2.6 collective-permute-start.9
  62.8 12.9 %expert_piece.4 = (bf16[48,4096]{1,0:T(8,128)(2,1)}, bf16[48,4096]{1,0:T(8,128)(2,1)}, bf16[48,4096]{1,0:T(8,128)(2,1)}, bf16[48,4096]{1,0:T(8,128)(2,1)}) custom-call(bf16[192,1536]{1,0:T(8,128)(2,1)} %bitcast.64, bf16[768,4096]{1,0:T(8,128)(2,1)} %bitcast.33, bf16[4096,768]{1,0:T(8,128)(2,1)} %bitcast.37, bf16[4096,768]{1,0:T(8,128)(2,1)} %bitcast.41, ...), custom_call_target="tpu_custom_call" | custom-call | tf_op jit(solution)/shard_map/expert_piece/pallas_call | solution.py:293
  75.8 2.3 collective-permute-done.8.refs_2_
  78.1 1.8 collective-permute-start.10
  81.8 3.4 %build_slots.6 = (bf16[48,4096]{1,0:T(8,128)(2,1)}, bf16[48,4096]{1,0:T(8,128)(2,1)}, bf16[48,4096]{1,0:T(8,128)(2,1)}, bf16[48,4096]{1,0:T(8,128)(2,1)}, f32[2,4,128]{2,1,0:T(4,128)}) custom-call(f32[192,2]{1,0:T(8,128)} %select_convert_fusion.ids_ref, bf16[128,4224]{1,0:T(8,128)(2,1)} %copy-done.4, bf16[128,4224]{1,0:T(8,128)(2,1)} %copy-done.7, ...), custom_call_target="tpu_custom_call" | custom-call | tf_op jit(solution)/shard_map/build_slots/pallas_call | solution.py:189
  88.7 12.8 %expert_piece.5 = (bf16[48,4096]{1,0:T(8,128)(2,1)}, bf16[48,4096]{1,0:T(8,128)(2,1)}, bf16[48,4096]{1,0:T(8,128)(2,1)}, bf16[48,4096]{1,0:T(8,128)(2,1)}) custom-call(bf16[192,1536]{1,0:T(8,128)(2,1)} %bitcast.63, bf16[768,4096]{1,0:T(8,128)(2,1)} %bitcast.34, bf16[4096,768]{1,0:T(8,128)(2,1)} %bitcast.38, bf16[4096,768]{1,0:T(8,128)(2,1)} %bitcast.42, ...), custom_call_target="tpu_custom_call" | custom-call | tf_op jit(solution)/shard_map/expert_piece/pallas_call | solution.py:293
  101.5 4.9 %collective-permute-done.10.own_x.own_ref = bf16[128,4224]{1,0:T(8,128)(2,1)S(1)} collective-permute-done((bf16[128,4224]{1,0:T(8,128)(2,1)S(1)}, bf16[128,4224]{1,0:T(8,128)(2,1)S(1)}, u32[]{:S(2)}, u32[]{:S(2)}) %collective-permute-start.10) | collective-permute-done | bytes 1081376 | tf_op jit(solution)/shard_map/ppermute | solution.py:30
  106.5 1.5 collective-permute-start.16
  110.0 6.4 %attention_core.6 = (bf16[128,1024]{1,0:T(8,128)(2,1)}, f32[1024,128]{1,0:T(8,128)}, f32[1024,128]{1,0:T(8,128)}) custom-call(f32[1024,128]{1,0:T(8,128)} %compare_select_fusion.bias_ref, bf16[128,4096]{1,0:T(8,128)(2,1)} %bitcast.55, bf16[128,4096]{1,0:T(8,128)(2,1)} %bitcast.59, bf16[1024,512]{1,0:T(8,128)(2,1)} %bitcast.49, bf16[1024,512]{1,0:T(8,128)(2,1)} %bitcast.50, ...), custom_call_target="tpu_custom_call" | custom-call | tf_op jit(solution)/shard_map/attention_core/pallas_call | solution.py:94
  117.5 3.5 %build_slots.7 = (bf16[48,4096]{1,0:T(8,128)(2,1)}, bf16[48,4096]{1,0:T(8,128)(2,1)}, bf16[48,4096]{1,0:T(8,128)(2,1)}, bf16[48,4096]{1,0:T(8,128)(2,1)}, f32[2,4,128]{2,1,0:T(4,128)}) custom-call(f32[192,2]{1,0:T(8,128)} %select_convert_fusion.ids_ref, bf16[128,4224]{1,0:T(8,128)(2,1)} %copy-done.5, bf16[128,4224]{1,0:T(8,128)(2,1)} %copy-done.6, ...), custom_call_target="tpu_custom_call" | custom-call | tf_op jit(solution)/shard_map/build_slots/pallas_call | solution.py:189
  121.0 6.4 %attention_core.7 = (bf16[128,1024]{1,0:T(8,128)(2,1)}, f32[1024,128]{1,0:T(8,128)}, f32[1024,128]{1,0:T(8,128)}) custom-call(f32[1024,128]{1,0:T(8,128)} %compare_select_fusion.bias_ref, bf16[128,4096]{1,0:T(8,128)(2,1)} %bitcast.56, bf16[128,4096]{1,0:T(8,128)(2,1)} %bitcast.60, bf16[1024,512]{1,0:T(8,128)(2,1)} %bitcast.51, bf16[1024,512]{1,0:T(8,128)(2,1)} %bitcast.52, ...), custom_call_target="tpu_custom_call" | custom-call | tf_op jit(solution)/shard_map/attention_core/pallas_call | solution.py:94
  128.7 3.5 %gather_tokens.4 = (f32[128,4096]{1,0:T(8,128)}, bf16[128,4096]{1,0:T(8,128)(2,1)}) custom-call(f32[192,2]{1,0:T(8,128)} %select_convert_fusion.ids_ref, f32[2,4,128]{2,1,0:T(4,128)} %get-tuple-element.136.meta_ref, bf16[48,4096]{1,0:T(8,128)(2,1)} %get-tuple-element.137.refs_0_, bf16[48,4096]{1,0:T(8,128)(2,1)} %copy-done.28, bf16[48,4096]{1,0:T(8,128)(2,1)} %copy-done.29, ...), custom_call_target="tpu_custom_call" | custom-call | tf_op jit(solution)/shard_map/gather_tokens/pallas_call | solution.py:227
  132.3 2.9 %collective-permute-done.22 = bf16[128,4096]{1,0:T(8,128)(2,1)S(1)} collective-permute-done((bf16[128,4096]{1,0:T(8,128)(2,1)}, bf16[128,4096]{1,0:T(8,128)(2,1)S(1)}, u32[]{:S(2)}, u32[]{:S(2)}) %collective-permute-start.22) | collective-permute-done | bytes 1048608 | tf_op jit(solution)/shard_map/ppermute | solution.py:25
  135.2 1.9 add_convert_fusion.3.refs_4_
  139.7 1.9 collective-permute-start.21
  141.6 12.7 %expert_piece.6 = (bf16[48,4096]{1,0:T(8,128)(2,1)}, bf16[48,4096]{1,0:T(8,128)(2,1)}, bf16[48,4096]{1,0:T(8,128)(2,1)}, bf16[48,4096]{1,0:T(8,128)(2,1)}) custom-call(bf16[192,1536]{1,0:T(8,128)(2,1)} %bitcast.62, bf16[768,4096]{1,0:T(8,128)(2,1)} %bitcast.35, bf16[4096,768]{1,0:T(8,128)(2,1)} %bitcast.39, bf16[4096,768]{1,0:T(8,128)(2,1)} %bitcast.43, ...), custom_call_target="tpu_custom_call" | custom-call | tf_op jit(solution)/shard_map/expert_piece/pallas_call | solution.py:293
  154.3 3.7 %collective-permute-done.20.refs_2_.refs_6_ = bf16[48,4096]{1,0:T(8,128)(2,1)S(1)} collective-permute-done((bf16[48,4096]{1,0:T(8,128)(2,1)S(1)}, bf16[48,4096]{1,0:T(8,128)(2,1)S(1)}, u32[]{:S(2)}, u32[]{:S(2)}) %collective-permute-start.20) | collective-permute-done | bytes 393248 | tf_op jit(solution)/shard_map/ppermute | solution.py:25
  159.8 1.8 collective-permute-start.25
  161.6 12.9 %expert_piece.7 = (bf16[48,4096]{1,0:T(8,128)(2,1)}, bf16[48,4096]{1,0:T(8,128)(2,1)}, bf16[48,4096]{1,0:T(8,128)(2,1)}, bf16[48,4096]{1,0:T(8,128)(2,1)}) custom-call(bf16[192,1536]{1,0:T(8,128)(2,1)} %bitcast.61, bf16[768,4096]{1,0:T(8,128)(2,1)} %bitcast.36, bf16[4096,768]{1,0:T(8,128)(2,1)} %bitcast.40, bf16[4096,768]{1,0:T(8,128)(2,1)} %bitcast.44, ...), custom_call_target="tpu_custom_call" | custom-call | tf_op jit(solution)/shard_map/expert_piece/pallas_call | solution.py:293
  178.1 3.7 %gather_tokens.5 = (f32[128,4096]{1,0:T(8,128)}, bf16[128,4096]{1,0:T(8,128)(2,1)}) custom-call(f32[192,2]{1,0:T(8,128)} %select_convert_fusion.ids_ref, f32[2,4,128]{2,1,0:T(4,128)} %get-tuple-element.160.meta_ref, bf16[48,4096]{1,0:T(8,128)(2,1)} %get-tuple-element.161.refs_4_.refs_0_, bf16[48,4096]{1,0:T(8,128)(2,1)} %copy-done.25, ...), custom_call_target="tpu_custom_call" | custom-call | tf_op jit(solution)/shard_map/gather_tokens/pallas_call | solution.py:227
  181.8 2.9 %collective-permute-done.33 = bf16[128,4096]{1,0:T(8,128)(2,1)S(1)} collective-permute-done((bf16[128,4096]{1,0:T(8,128)(2,1)}, bf16[128,4096]{1,0:T(8,128)(2,1)S(1)}, u32[]{:S(2)}, u32[]{:S(2)}) %collective-permute-start.33) | collective-permute-done | bytes 1048608 | tf_op jit(solution)/shard_map/ppermute | solution.py:25
  184.7 1.9 add_convert_fusion.2.refs_5_
  188.0 1.5 collective-permute-start.27
  190.6 8.5 %collective-permute-done.26.refs_1_ = bf16[48,4096]{1,0:T(8,128)(2,1)S(1)} collective-permute-done((bf16[48,4096]{1,0:T(8,128)(2,1)S(1)}, bf16[48,4096]{1,0:T(8,128)(2,1)S(1)}, u32[]{:S(2)}, u32[]{:S(2)}) %collective-permute-start.26) | collective-permute-done | bytes 393248 | tf_op jit(solution)/shard_map/ppermute | solution.py:25
  199.1 7.0 %collective-permute-done.27.refs_2_ = bf16[48,4096]{1,0:T(8,128)(2,1)S(1)} collective-permute-done((bf16[48,4096]{1,0:T(8,128)(2,1)S(1)}, bf16[48,4096]{1,0:T(8,128)(2,1)S(1)}, u32[]{:S(2)}, u32[]{:S(2)}) %collective-permute-start.27) | collective-permute-done | bytes 393248 | tf_op jit(solution)/shard_map/ppermute | solution.py:25
  207.1 6.5 %collective-permute-done.34.refs_4_ = bf16[128,4096]{1,0:T(8,128)(2,1)S(1)} collective-permute-done((bf16[128,4096]{1,0:T(8,128)(2,1)S(1)}, bf16[128,4096]{1,0:T(8,128)(2,1)S(1)}, u32[]{:S(2)}, u32[]{:S(2)}) %collective-permute-start.34) | collective-permute-done | bytes 1048608 | tf_op jit(solution)/shard_map/ppermute | solution.py:30
  214.6 4.0 %gather_tokens.6 = (f32[128,4096]{1,0:T(8,128)}, bf16[128,4096]{1,0:T(8,128)(2,1)}) custom-call(f32[192,2]{1,0:T(8,128)} %select_convert_fusion.ids_ref, f32[2,4,128]{2,1,0:T(4,128)} %get-tuple-element.158.meta_ref, bf16[48,4096]{1,0:T(8,128)(2,1)} %get-tuple-element.159.refs_5_.refs_0_, bf16[48,4096]{1,0:T(8,128)(2,1)} %copy-done.31, ...), custom_call_target="tpu_custom_call" | custom-call | tf_op jit(solution)/shard_map/gather_tokens/pallas_call | solution.py:227
  218.6 2.9 %collective-permute-done.35 = bf16[128,4096]{1,0:T(8,128)(2,1)S(1)} collective-permute-done((bf16[128,4096]{1,0:T(8,128)(2,1)}, bf16[128,4096]{1,0:T(8,128)(2,1)S(1)}, u32[]{:S(2)}, u32[]{:S(2)}) %collective-permute-start.35) | collective-permute-done | bytes 1048608 | tf_op jit(solution)/shard_map/ppermute | solution.py:25
  221.5 1.9 add_convert_fusion.1.refs_5_
  224.4 1.5 collective-permute-start.30
  228.3 3.6 %all-to-all-start.1 = ((bf16[8,128,512]{2,1,0:T(8,128)(2,1)}), bf16[8,128,512]{2,1,0:T(8,128)(2,1)S(1)}, u32[]{:S(2)}, u32[]{:S(2)}) async-start(bf16[8,128,512]{2,1,0:T(8,128)(2,1)} %pad_maximum_fusion), calls=%async_computation.1 | async-start | bytes 2097152 | tf_op jit(solution)/shard_map/all_to_all | solution.py:485
  231.9 3.9 %collective-permute-done.29.refs_1_ = bf16[48,4096]{1,0:T(8,128)(2,1)} collective-permute-done((bf16[48,4096]{1,0:T(8,128)(2,1)}, bf16[48,4096]{1,0:T(8,128)(2,1)}, u32[]{:S(2)}, u32[]{:S(2)}) %collective-permute-start.29) | collective-permute-done | bytes 393248 | tf_op jit(solution)/shard_map/ppermute | solution.py:25
  235.8 8.4 %collective-permute-done.30.refs_2_ = bf16[48,4096]{1,0:T(8,128)(2,1)} collective-permute-done((bf16[48,4096]{1,0:T(8,128)(2,1)}, bf16[48,4096]{1,0:T(8,128)(2,1)}, u32[]{:S(2)}, u32[]{:S(2)}) %collective-permute-start.30) | collective-permute-done | bytes 393248 | tf_op jit(solution)/shard_map/ppermute | solution.py:25
  245.0 5.4 %collective-permute-done.36.refs_4_ = bf16[128,4096]{1,0:T(8,128)(2,1)S(1)} collective-permute-done((bf16[128,4096]{1,0:T(8,128)(2,1)S(1)}, bf16[128,4096]{1,0:T(8,128)(2,1)S(1)}, u32[]{:S(2)}, u32[]{:S(2)}) %collective-permute-start.36) | collective-permute-done | bytes 1048608 | tf_op jit(solution)/shard_map/ppermute | solution.py:30
  251.4 3.8 %gather_tokens.7 = (f32[128,4096]{1,0:T(8,128)}, bf16[128,4096]{1,0:T(8,128)(2,1)}) custom-call(f32[192,2]{1,0:T(8,128)} %select_convert_fusion.ids_ref, f32[2,4,128]{2,1,0:T(4,128)} %get-tuple-element.119.meta_ref, bf16[48,4096]{1,0:T(8,128)(2,1)} %get-tuple-element.154.refs_0_, bf16[48,4096]{1,0:T(8,128)(2,1)} %collective-permute-done.29.refs_1_, ...), custom_call_target="tpu_custom_call" | custom-call | tf_op jit(solution)/shard_map/gather_tokens/pallas_call | solution.py:227
  258.1 2.9 %fusion = bf16[1,128,4096]{2,1,0:T(8,128)(2,1)} fusion(f32[128,4096]{1,0:T(8,128)} %get-tuple-element.166, bf16[128,4096]{1,0:T(8,128)(2,1)S(1)} %collective-permute-done.37), kind=kLoop, calls=%fused_computation.5 | loop fusion | flops 1572864 | bytes 4194304 | tf_op jit(solution)/shard_map/broadcast_in_dim | solution.py:477
  (182 shorter events, 38.8 us)
Async XLA Ops:
  0.6 45.2 %copy-start = (bf16[1,32,24,1536]{3,2,1,0:T(8,128)(2,1)S(1)}, bf16[1,32,24,1536]{3,2,1,0:T(8,128)(2,1)}, u32[]{:S(2)}) copy-start(bf16[1,32,24,1536]{3,2,1,0:T(8,128)(2,1)} %param.23) | copy-start | bytes 7077892
  3.2 31.4 %collective-permute-start.1 = (bf16[128,4224]{1,0:T(8,128)(2,1)}, bf16[128,4224]{1,0:T(8,128)(2,1)}, u32[]{:S(2)}, u32[]{:S(2)}) collective-permute-start(bf16[128,4224]{1,0:T(8,128)(2,1)} %pack_tokens.1.own_x.own_ref), channel_id=1, source_target_pairs={{0,1},{1,2},{2,3},{3,0},{4,5},{5,6},{6,7},{7,4},{8,9},{9,10},{10,1... | collective-permute-start | bytes 3244040 | tf_op jit(solution)/shard_map/ppermute | solution.py:30
  6.2 6.1 %collective-permute-start = (bf16[128,4224]{1,0:T(8,128)(2,1)}, bf16[128,4224]{1,0:T(8,128)(2,1)}, u32[]{:S(2)}, u32[]{:S(2)}) collective-permute-start(bf16[128,4224]{1,0:T(8,128)(2,1)} %pack_tokens.1.own_x.own_ref), channel_id=1, source_target_pairs={{0,4},{4,0},{8,12},{12,8},{16,20},{20,16},{24,28},{28,24},{1,5},{5... | collective-permute-start | bytes 3244040 | tf_op jit(solution)/shard_map/ppermute | solution.py:25
  7.3 19.8 %all-to-all-start = ((bf16[8,128,512]{2,1,0:T(8,128)(2,1)}), bf16[8,128,512]{2,1,0:T(8,128)(2,1)S(1)}, u32[]{:S(2)}, u32[]{:S(2)}) async-start(bf16[8,128,512]{2,1,0:T(8,128)(2,1)} %broadcast_in_dim.104), calls=%async_computation | async-start | bytes 2097152 | tf_op jit(solution)/shard_map/all_to_all | solution.py:351
  15.6 19.1 %collective-permute-start.2 = (bf16[48,4096]{1,0:T(8,128)(2,1)}, bf16[48,4096]{1,0:T(8,128)(2,1)}, u32[]{:S(2)}, u32[]{:S(2)}) collective-permute-start(bf16[48,4096]{1,0:T(8,128)(2,1)} %get-tuple-element.90), channel_id=1, source_target_pairs={{0,8},{4,12},{8,0},{12,4},{16,24},{20,28},{24,16},{28,20},{1,9},{5... | collective-permute-start | bytes 1179656 | tf_op jit(solution)/shard_map/ppermute | solution.py:25
  17.6 17.1 %collective-permute-start.3 = (bf16[48,4096]{1,0:T(8,128)(2,1)}, bf16[48,4096]{1,0:T(8,128)(2,1)}, u32[]{:S(2)}, u32[]{:S(2)}) collective-permute-start(bf16[48,4096]{1,0:T(8,128)(2,1)} %get-tuple-element.91), channel_id=1, source_target_pairs={{0,16},{4,20},{8,24},{12,28},{16,0},{20,4},{24,8},{28,12},{1,17},{... | collective-permute-start | bytes 1179656 | tf_op jit(solution)/shard_map/ppermute | solution.py:25
  19.1 24.5 %collective-permute-start.4 = (bf16[48,4096]{1,0:T(8,128)(2,1)}, bf16[48,4096]{1,0:T(8,128)(2,1)}, u32[]{:S(2)}, u32[]{:S(2)}) collective-permute-start(bf16[48,4096]{1,0:T(8,128)(2,1)} %get-tuple-element.92), channel_id=1, source_target_pairs={{0,24},{4,28},{8,16},{12,20},{16,8},{20,12},{24,0},{28,4},{1,25},{... | collective-permute-start | bytes 1179656 | tf_op jit(solution)/shard_map/ppermute | solution.py:25
  43.5 10.9 %collective-permute-start.6 = (bf16[128,4224]{1,0:T(8,128)(2,1)}, bf16[128,4224]{1,0:T(8,128)(2,1)}, u32[]{:S(2)}, u32[]{:S(2)}) collective-permute-start(bf16[128,4224]{1,0:T(8,128)(2,1)} %collective-permute-done.1.own_x.own_ref), channel_id=1, source_target_pairs={{0,4},{4,0},{8,12},{12,8},{16,20},{20,16},{24,28},{28,24},{1,5},{5... | collective-permute-start | bytes 3244040 | tf_op jit(solution)/shard_map/ppermute | solution.py:25
  43.5 32.2 %collective-permute-start.5 = (bf16[128,4224]{1,0:T(8,128)(2,1)}, bf16[128,4224]{1,0:T(8,128)(2,1)S(1)}, u32[]{:S(2)}, u32[]{:S(2)}) collective-permute-start(bf16[128,4224]{1,0:T(8,128)(2,1)} %collective-permute-done.1.own_x.own_ref), channel_id=1, source_target_pairs={{0,1},{1,2},{2,3},{3,0},{4,5},{5,6},{6,7},{7,4},{8,9},{9,10},{10,1... | collective-permute-start | bytes 3244040 | tf_op jit(solution)/shard_map/ppermute | solution.py:30
  57.9 17.9 %collective-permute-start.7 = (bf16[48,4096]{1,0:T(8,128)(2,1)}, bf16[48,4096]{1,0:T(8,128)(2,1)S(1)}, u32[]{:S(2)}, u32[]{:S(2)}) collective-permute-start(bf16[48,4096]{1,0:T(8,128)(2,1)} %get-tuple-element.98), channel_id=1, source_target_pairs={{0,8},{4,12},{8,0},{12,4},{16,24},{20,28},{24,16},{28,20},{1,9},{5... | collective-permute-start | bytes 1179656 | tf_op jit(solution)/shard_map/ppermute | solution.py:25
  58.4 19.6 %collective-permute-start.8 = (bf16[48,4096]{1,0:T(8,128)(2,1)}, bf16[48,4096]{1,0:T(8,128)(2,1)S(1)}, u32[]{:S(2)}, u32[]{:S(2)}) collective-permute-start(bf16[48,4096]{1,0:T(8,128)(2,1)} %get-tuple-element.99), channel_id=1, source_target_pairs={{0,16},{4,20},{8,24},{12,28},{16,0},{20,4},{24,8},{28,12},{1,17},{... | collective-permute-start | bytes 1179656 | tf_op jit(solution)/shard_map/ppermute | solution.py:25
  58.8 19.2 %collective-permute-start.9 = (bf16[48,4096]{1,0:T(8,128)(2,1)}, bf16[48,4096]{1,0:T(8,128)(2,1)S(1)}, u32[]{:S(2)}, u32[]{:S(2)}) collective-permute-start(bf16[48,4096]{1,0:T(8,128)(2,1)} %get-tuple-element.100), channel_id=1, source_target_pairs={{0,24},{4,28},{8,16},{12,20},{16,8},{20,12},{24,0},{28,4},{1,25},{... | collective-permute-start | bytes 1179656 | tf_op jit(solution)/shard_map/ppermute | solution.py:25
  75.8 12.9 %copy-start.37 = (bf16[48,4096]{1,0:T(8,128)(2,1)}, bf16[48,4096]{1,0:T(8,128)(2,1)S(1)}, u32[]{:S(2)}) copy-start(bf16[48,4096]{1,0:T(8,128)(2,1)S(1)} %collective-permute-done.7.refs_1_) | copy-start | bytes 1179652
  78.1 2.8 %collective-permute-start.11 = (bf16[128,4224]{1,0:T(8,128)(2,1)S(1)}, bf16[128,4224]{1,0:T(8,128)(2,1)S(1)}, u32[]{:S(2)}, u32[]{:S(2)}) collective-permute-start(bf16[128,4224]{1,0:T(8,128)(2,1)S(1)} %collective-permute-done.5.own_x.own_ref), channel_id=1, source_target_pairs={{0,4},{4,0},{8,12},{12,8},{16,20},{20,16},{24,28},{28,24},{1,5},{5... | collective-permute-start | bytes 3244040 | tf_op jit(solution)/shard_map/ppermute | solution.py:25
  78.1 28.2 %collective-permute-start.10 = (bf16[128,4224]{1,0:T(8,128)(2,1)S(1)}, bf16[128,4224]{1,0:T(8,128)(2,1)S(1)}, u32[]{:S(2)}, u32[]{:S(2)}) collective-permute-start(bf16[128,4224]{1,0:T(8,128)(2,1)S(1)} %collective-permute-done.5.own_x.own_ref), channel_id=1, source_target_pairs={{0,1},{1,2},{2,3},{3,0},{4,5},{5,6},{6,7},{7,4},{8,9},{9,10},{10,1... | collective-permute-start | bytes 3244040 | tf_op jit(solution)/shard_map/ppermute | solution.py:30
  85.2 21.2 %collective-permute-start.12 = (bf16[48,4096]{1,0:T(8,128)(2,1)}, bf16[48,4096]{1,0:T(8,128)(2,1)S(1)}, u32[]{:S(2)}, u32[]{:S(2)}) collective-permute-start(bf16[48,4096]{1,0:T(8,128)(2,1)} %get-tuple-element.105), channel_id=1, source_target_pairs={{0,8},{4,12},{8,0},{12,4},{16,24},{20,28},{24,16},{28,20},{1,9},{5... | collective-permute-start | bytes 1179656 | tf_op jit(solution)/shard_map/ppermute | solution.py:25
  86.6 19.7 %collective-permute-start.13 = (bf16[48,4096]{1,0:T(8,128)(2,1)}, bf16[48,4096]{1,0:T(8,128)(2,1)S(1)}, u32[]{:S(2)}, u32[]{:S(2)}) collective-permute-start(bf16[48,4096]{1,0:T(8,128)(2,1)} %get-tuple-element.106), channel_id=1, source_target_pairs={{0,16},{4,20},{8,24},{12,28},{16,0},{20,4},{24,8},{28,12},{1,17},{... | collective-permute-start | bytes 1179656 | tf_op jit(solution)/shard_map/ppermute | solution.py:25
  87.2 19.2 %collective-permute-start.14 = (bf16[48,4096]{1,0:T(8,128)(2,1)}, bf16[48,4096]{1,0:T(8,128)(2,1)S(1)}, u32[]{:S(2)}, u32[]{:S(2)}) collective-permute-start(bf16[48,4096]{1,0:T(8,128)(2,1)} %get-tuple-element.107), channel_id=1, source_target_pairs={{0,24},{4,28},{8,16},{12,20},{16,8},{20,12},{24,0},{28,4},{1,25},{... | collective-permute-start | bytes 1179656 | tf_op jit(solution)/shard_map/ppermute | solution.py:25
  106.4 10.1 %collective-permute-start.15 = (bf16[128,4224]{1,0:T(8,128)(2,1)S(1)}, bf16[128,4224]{1,0:T(8,128)(2,1)S(1)}, u32[]{:S(2)}, u32[]{:S(2)}) collective-permute-start(bf16[128,4224]{1,0:T(8,128)(2,1)S(1)} %collective-permute-done.10.own_x.own_ref), channel_id=1, source_target_pairs={{0,4},{4,0},{8,12},{12,8},{16,20},{20,16},{24,28},{28,24},{1,5},{5... | collective-permute-start | bytes 3244040 | tf_op jit(solution)/shard_map/ppermute | solution.py:25
  106.5 20.9 %collective-permute-start.16 = (bf16[48,4096]{1,0:T(8,128)(2,1)}, bf16[48,4096]{1,0:T(8,128)(2,1)S(1)}, u32[]{:S(2)}, u32[]{:S(2)}) collective-permute-start(bf16[48,4096]{1,0:T(8,128)(2,1)} %get-tuple-element.129), channel_id=1, source_target_pairs={{0,8},{4,12},{8,0},{12,4},{16,24},{20,28},{24,16},{28,20},{1,9},{5... | collective-permute-start | bytes 1179656 | tf_op jit(solution)/shard_map/ppermute | solution.py:25
  108.0 19.8 %collective-permute-start.17 = (bf16[48,4096]{1,0:T(8,128)(2,1)}, bf16[48,4096]{1,0:T(8,128)(2,1)S(1)}, u32[]{:S(2)}, u32[]{:S(2)}) collective-permute-start(bf16[48,4096]{1,0:T(8,128)(2,1)} %get-tuple-element.130), channel_id=1, source_target_pairs={{0,16},{4,20},{8,24},{12,28},{16,0},{20,4},{24,8},{28,12},{1,17},{... | collective-permute-start | bytes 1179656 | tf_op jit(solution)/shard_map/ppermute | solution.py:25
  108.6 19.3 %collective-permute-start.18 = (bf16[48,4096]{1,0:T(8,128)(2,1)}, bf16[48,4096]{1,0:T(8,128)(2,1)S(1)}, u32[]{:S(2)}, u32[]{:S(2)}) collective-permute-start(bf16[48,4096]{1,0:T(8,128)(2,1)} %get-tuple-element.131), channel_id=1, source_target_pairs={{0,24},{4,28},{8,16},{12,20},{16,8},{20,12},{24,0},{28,4},{1,25},{... | collective-permute-start | bytes 1179656 | tf_op jit(solution)/shard_map/ppermute | solution.py:25
  132.3 2.9 %collective-permute-start.22 = (bf16[128,4096]{1,0:T(8,128)(2,1)}, bf16[128,4096]{1,0:T(8,128)(2,1)S(1)}, u32[]{:S(2)}, u32[]{:S(2)}) collective-permute-start(bf16[128,4096]{1,0:T(8,128)(2,1)} %get-tuple-element.139), channel_id=1, source_target_pairs={{0,4},{4,0},{8,12},{12,8},{16,20},{20,16},{24,28},{28,24},{1,5},{5... | collective-permute-start | bytes 3145736 | tf_op jit(solution)/shard_map/ppermute | solution.py:25
  137.1 39.9 %collective-permute-start.32 = (bf16[128,4096]{1,0:T(8,128)(2,1)S(1)}, bf16[128,4096]{1,0:T(8,128)(2,1)S(1)}, u32[]{:S(2)}, u32[]{:S(2)}) collective-permute-start(bf16[128,4096]{1,0:T(8,128)(2,1)S(1)} %add_convert_fusion.3.refs_4_), channel_id=1, source_target_pairs={{0,1},{1,2},{2,3},{3,0},{4,5},{5,6},{6,7},{7,4},{8,9},{9,10},{10,1... | collective-permute-start | bytes 3145736 | tf_op jit(solution)/shard_map/ppermute | solution.py:30
  138.1 16.2 %collective-permute-start.19 = (bf16[48,4096]{1,0:T(8,128)(2,1)S(1)}, bf16[48,4096]{1,0:T(8,128)(2,1)S(1)}, u32[]{:S(2)}, u32[]{:S(2)}) collective-permute-start(bf16[48,4096]{1,0:T(8,128)(2,1)S(1)} %copy-done.45), channel_id=1, source_target_pairs={{0,8},{4,12},{8,0},{12,4},{16,24},{20,28},{24,16},{28,20},{1,9},{5... | collective-permute-start | bytes 1179656 | tf_op jit(solution)/shard_map/ppermute | solution.py:25
  139.0 19.0 %collective-permute-start.20 = (bf16[48,4096]{1,0:T(8,128)(2,1)S(1)}, bf16[48,4096]{1,0:T(8,128)(2,1)S(1)}, u32[]{:S(2)}, u32[]{:S(2)}) collective-permute-start(bf16[48,4096]{1,0:T(8,128)(2,1)S(1)} %copy-done.44), channel_id=1, source_target_pairs={{0,16},{4,20},{8,24},{12,28},{16,0},{20,4},{24,8},{28,12},{1,17},{... | collective-permute-start | bytes 1179656 | tf_op jit(solution)/shard_map/ppermute | solution.py:25
  139.7 18.3 %collective-permute-start.21 = (bf16[48,4096]{1,0:T(8,128)(2,1)S(1)}, bf16[48,4096]{1,0:T(8,128)(2,1)S(1)}, u32[]{:S(2)}, u32[]{:S(2)}) collective-permute-start(bf16[48,4096]{1,0:T(8,128)(2,1)S(1)} %copy-done.43), channel_id=1, source_target_pairs={{0,24},{4,28},{8,16},{12,20},{16,8},{20,12},{24,0},{28,4},{1,25},{... | collective-permute-start | bytes 1179656 | tf_op jit(solution)/shard_map/ppermute | solution.py:25
  158.1 16.5 %collective-permute-start.23 = (bf16[48,4096]{1,0:T(8,128)(2,1)}, bf16[48,4096]{1,0:T(8,128)(2,1)S(1)}, u32[]{:S(2)}, u32[]{:S(2)}) collective-permute-start(bf16[48,4096]{1,0:T(8,128)(2,1)} %get-tuple-element.148), channel_id=1, source_target_pairs={{0,8},{4,12},{8,0},{12,4},{16,24},{20,28},{24,16},{28,20},{1,9},{5... | collective-permute-start | bytes 1179656 | tf_op jit(solution)/shard_map/ppermute | solution.py:25
  159.2 16.6 %collective-permute-start.24 = (bf16[48,4096]{1,0:T(8,128)(2,1)}, bf16[48,4096]{1,0:T(8,128)(2,1)S(1)}, u32[]{:S(2)}, u32[]{:S(2)}) collective-permute-start(bf16[48,4096]{1,0:T(8,128)(2,1)} %get-tuple-element.149), channel_id=1, source_target_pairs={{0,16},{4,20},{8,24},{12,28},{16,0},{20,4},{24,8},{28,12},{1,17},{... | collective-permute-start | bytes 1179656 | tf_op jit(solution)/shard_map/ppermute | solution.py:25
  159.8 17.2 %collective-permute-start.25 = (bf16[48,4096]{1,0:T(8,128)(2,1)}, bf16[48,4096]{1,0:T(8,128)(2,1)S(1)}, u32[]{:S(2)}, u32[]{:S(2)}) collective-permute-start(bf16[48,4096]{1,0:T(8,128)(2,1)} %get-tuple-element.150), channel_id=1, source_target_pairs={{0,24},{4,28},{8,16},{12,20},{16,8},{20,12},{24,0},{28,4},{1,25},{... | collective-permute-start | bytes 1179656 | tf_op jit(solution)/shard_map/ppermute | solution.py:25
  181.8 2.9 %collective-permute-start.33 = (bf16[128,4096]{1,0:T(8,128)(2,1)}, bf16[128,4096]{1,0:T(8,128)(2,1)S(1)}, u32[]{:S(2)}, u32[]{:S(2)}) collective-permute-start(bf16[128,4096]{1,0:T(8,128)(2,1)} %get-tuple-element.163), channel_id=1, source_target_pairs={{0,4},{4,0},{8,12},{12,8},{16,20},{20,16},{24,28},{28,24},{1,5},{5... | collective-permute-start | bytes 3145736 | tf_op jit(solution)/shard_map/ppermute | solution.py:25
  186.6 27.1 %copy-start.9 = (bf16[128,4096]{1,0:T(8,128)(2,1)}, bf16[128,4096]{1,0:T(8,128)(2,1)S(1)}, u32[]{:S(2)}) copy-start(bf16[128,4096]{1,0:T(8,128)(2,1)S(1)} %add_convert_fusion.2.refs_5_) | copy-start | bytes 3145732
  186.6 27.1 %collective-permute-start.34 = (bf16[128,4096]{1,0:T(8,128)(2,1)S(1)}, bf16[128,4096]{1,0:T(8,128)(2,1)S(1)}, u32[]{:S(2)}, u32[]{:S(2)}) collective-permute-start(bf16[128,4096]{1,0:T(8,128)(2,1)S(1)} %add_convert_fusion.2.refs_5_), channel_id=1, source_target_pairs={{0,1},{1,2},{2,3},{3,0},{4,5},{5,6},{6,7},{7,4},{8,9},{9,10},{10,1... | collective-permute-start | bytes 3145736 | tf_op jit(solution)/shard_map/ppermute | solution.py:30
  187.1 12.0 %collective-permute-start.26 = (bf16[48,4096]{1,0:T(8,128)(2,1)S(1)}, bf16[48,4096]{1,0:T(8,128)(2,1)S(1)}, u32[]{:S(2)}, u32[]{:S(2)}) collective-permute-start(bf16[48,4096]{1,0:T(8,128)(2,1)S(1)} %copy-done.48), channel_id=1, source_target_pairs={{0,8},{4,12},{8,0},{12,4},{16,24},{20,28},{24,16},{28,20},{1,9},{5... | collective-permute-start | bytes 1179656 | tf_op jit(solution)/shard_map/ppermute | solution.py:25
  188.0 18.1 %collective-permute-start.27 = (bf16[48,4096]{1,0:T(8,128)(2,1)S(1)}, bf16[48,4096]{1,0:T(8,128)(2,1)S(1)}, u32[]{:S(2)}, u32[]{:S(2)}) collective-permute-start(bf16[48,4096]{1,0:T(8,128)(2,1)S(1)} %copy-done.47), channel_id=1, source_target_pairs={{0,16},{4,20},{8,24},{12,28},{16,0},{20,4},{24,8},{28,12},{1,17},{... | collective-permute-start | bytes 1179656 | tf_op jit(solution)/shard_map/ppermute | solution.py:25
  189.5 17.6 %collective-permute-start.28 = (bf16[48,4096]{1,0:T(8,128)(2,1)S(1)}, bf16[48,4096]{1,0:T(8,128)(2,1)S(1)}, u32[]{:S(2)}, u32[]{:S(2)}) collective-permute-start(bf16[48,4096]{1,0:T(8,128)(2,1)S(1)} %copy-done.46), channel_id=1, source_target_pairs={{0,24},{4,28},{8,16},{12,20},{16,8},{20,12},{24,0},{28,4},{1,25},{... | collective-permute-start | bytes 1179656 | tf_op jit(solution)/shard_map/ppermute | solution.py:25
  199.1 14.6 %copy-start.31 = (bf16[48,4096]{1,0:T(8,128)(2,1)}, bf16[48,4096]{1,0:T(8,128)(2,1)S(1)}, u32[]{:S(2)}) copy-start(bf16[48,4096]{1,0:T(8,128)(2,1)S(1)} %collective-permute-done.26.refs_1_) | copy-start | bytes 1179652
  218.6 2.9 %collective-permute-start.35 = (bf16[128,4096]{1,0:T(8,128)(2,1)}, bf16[128,4096]{1,0:T(8,128)(2,1)S(1)}, u32[]{:S(2)}, u32[]{:S(2)}) collective-permute-start(bf16[128,4096]{1,0:T(8,128)(2,1)} %get-tuple-element.165), channel_id=1, source_target_pairs={{0,4},{4,0},{8,12},{12,8},{16,20},{20,16},{24,28},{28,24},{1,5},{5... | collective-permute-start | bytes 3145736 | tf_op jit(solution)/shard_map/ppermute | solution.py:25
  223.4 27.1 %collective-permute-start.36 = (bf16[128,4096]{1,0:T(8,128)(2,1)S(1)}, bf16[128,4096]{1,0:T(8,128)(2,1)S(1)}, u32[]{:S(2)}, u32[]{:S(2)}) collective-permute-start(bf16[128,4096]{1,0:T(8,128)(2,1)S(1)} %add_convert_fusion.1.refs_5_), channel_id=1, source_target_pairs={{0,1},{1,2},{2,3},{3,0},{4,5},{5,6},{6,7},{7,4},{8,9},{9,10},{10,1... | collective-permute-start | bytes 3145736 | tf_op jit(solution)/shard_map/ppermute | solution.py:30
  223.5 12.3 %collective-permute-start.29 = (bf16[48,4096]{1,0:T(8,128)(2,1)}, bf16[48,4096]{1,0:T(8,128)(2,1)}, u32[]{:S(2)}, u32[]{:S(2)}) collective-permute-start(bf16[48,4096]{1,0:T(8,128)(2,1)} %get-tuple-element.155), channel_id=1, source_target_pairs={{0,8},{4,12},{8,0},{12,4},{16,24},{20,28},{24,16},{28,20},{1,9},{5... | collective-permute-start | bytes 1179656 | tf_op jit(solution)/shard_map/ppermute | solution.py:25
  224.4 19.8 %collective-permute-start.30 = (bf16[48,4096]{1,0:T(8,128)(2,1)}, bf16[48,4096]{1,0:T(8,128)(2,1)}, u32[]{:S(2)}, u32[]{:S(2)}) collective-permute-start(bf16[48,4096]{1,0:T(8,128)(2,1)} %get-tuple-element.156), channel_id=1, source_target_pairs={{0,16},{4,20},{8,24},{12,28},{16,0},{20,4},{24,8},{28,12},{1,17},{... | collective-permute-start | bytes 1179656 | tf_op jit(solution)/shard_map/ppermute | solution.py:25
  226.0 19.1 %collective-permute-start.31 = (bf16[48,4096]{1,0:T(8,128)(2,1)}, bf16[48,4096]{1,0:T(8,128)(2,1)}, u32[]{:S(2)}, u32[]{:S(2)}) collective-permute-start(bf16[48,4096]{1,0:T(8,128)(2,1)} %get-tuple-element.157), channel_id=1, source_target_pairs={{0,24},{4,28},{8,16},{12,20},{16,8},{20,12},{24,0},{28,4},{1,25},{... | collective-permute-start | bytes 1179656 | tf_op jit(solution)/shard_map/ppermute | solution.py:25
  228.3 28.0 %all-to-all-start.1 = ((bf16[8,128,512]{2,1,0:T(8,128)(2,1)}), bf16[8,128,512]{2,1,0:T(8,128)(2,1)S(1)}, u32[]{:S(2)}, u32[]{:S(2)}) async-start(bf16[8,128,512]{2,1,0:T(8,128)(2,1)} %pad_maximum_fusion), calls=%async_computation.1 | async-start | bytes 2097152 | tf_op jit(solution)/shard_map/all_to_all | solution.py:485
  231.9 23.3 %copy-start.17 = (bf16[128,1024]{1,0:T(8,128)(2,1)S(1)}, bf16[128,1024]{1,0:T(8,128)(2,1)}, u32[]{:S(2)}) copy-start(bf16[128,1024]{1,0:T(8,128)(2,1)} %get-tuple-element.93.refs_0_) | copy-start | bytes 786436
  231.9 23.3 %copy-start.18 = (bf16[128,1024]{1,0:T(8,128)(2,1)S(1)}, bf16[128,1024]{1,0:T(8,128)(2,1)}, u32[]{:S(2)}) copy-start(bf16[128,1024]{1,0:T(8,128)(2,1)} %get-tuple-element.94.refs_0_) | copy-start | bytes 786436
  231.9 23.3 %copy-start.19 = (bf16[128,1024]{1,0:T(8,128)(2,1)S(1)}, bf16[128,1024]{1,0:T(8,128)(2,1)}, u32[]{:S(2)}) copy-start(bf16[128,1024]{1,0:T(8,128)(2,1)} %get-tuple-element.109.refs_0_) | copy-start | bytes 786436
  231.9 23.3 %copy-start.20 = (bf16[128,1024]{1,0:T(8,128)(2,1)S(1)}, bf16[128,1024]{1,0:T(8,128)(2,1)}, u32[]{:S(2)}) copy-start(bf16[128,1024]{1,0:T(8,128)(2,1)} %get-tuple-element.114.refs_4_) | copy-start | bytes 786436
  255.2 2.9 %collective-permute-start.37 = (bf16[128,4096]{1,0:T(8,128)(2,1)}, bf16[128,4096]{1,0:T(8,128)(2,1)S(1)}, u32[]{:S(2)}, u32[]{:S(2)}) collective-permute-start(bf16[128,4096]{1,0:T(8,128)(2,1)} %get-tuple-element.167), channel_id=1, source_target_pairs={{0,4},{4,0},{8,12},{12,8},{16,20},{20,16},{24,28},{28,24},{1,5},{5... | collective-permute-start | bytes 3145736 | tf_op jit(solution)/shard_map/ppermute | solution.py:25
  (41 other events, 190.0 us)
where the time goes:
time: 266 us; the launch traced here: 261 us
  Pallas kernels  108 us (41%)
  waiting for transfers between devices  81.6 us (31%)
  starting transfers between devices  44.2 us (17%)
  other arithmetic  13.2 us (5%)
  local copies, waits for them, and re-layouts  12.7 us (5%)
    ppermute x32, waiting for transfers between devices, swap(): return lax.ppermute(value, 'ctx', [(i, i ^ mask) for i in range(count)])  58 us
    pallas_call x4, Pallas kernels, expert(): pl.pallas_call(functools.partial(expert_kernel, count, half, len(after)),...  51.3 us
    ppermute x32, starting transfers between devices, swap(): return lax.ppermute(value, 'ctx', [(i, i ^ mask) for i in range(count)])  28.3 us
    pallas_call x4, Pallas kernels, attention(): pl.pallas_call(functools.partial(attention_kernel, after=len(after)), gri...  25.6 us
    ppermute x6, waiting for transfers between devices, turn(): lax.ppermute(value, 'exp', [(i, (i + steps) % count) for i in range(count)])  16.7 us
    pallas_call x4, Pallas kernels, gather_tokens(): pl.pallas_call(functools.partial(tokens_kernel, len(pieces), len(received...  15 us
    pallas_call x4, Pallas kernels, build_slots(): pl.pallas_call(functools.partial(slots_kernel, capacity, len(after)), gri...  13.7 us
    ppermute x6, starting transfers between devices, turn(): lax.ppermute(value, 'exp', [(i, (i + steps) % count) for i in range(count)])  8.5 us
  transfers between devices with their start and end apart: 40, of which 22 were waited for; matrix products, arithmetic and copies ran while one was open for 4% of the time, Pallas kernels for 36%

commit v1 on v0

--- a/solution.py
+++ b/solution.py
@@ -206,16 +206,15 @@
 
 
 def tokens_kernel(count, adds, ids_ref, meta_ref, *refs):
-    pieces, (own_ref, other_ref) = refs[:count], refs[-2:]
+    pieces, out = refs[:count], refs[-1]
     rows = jnp.concatenate([piece[...] for piece in pieces], axis=0)
-    for rel, out in ((1, other_ref), (0, own_ref)):
-        ids = ids_ref[:, rel : rel + 1]
-        place = (meta_ref[rel, 0:1, :] == ids) | (meta_ref[rel, 1:2, :] == ids)
-        place = jnp.where(place, 1.0, 0.0).astype(jnp.bfloat16)
-        total = rows_dot(place, rows, ((0,), (0,)))
-        if adds and rel == 0:
-            total = total + refs[count][...].astype(jnp.float32)
-        out[...] = total.astype(out.dtype)
+    ids = ids_ref[...]
+    place = (meta_ref[0, 0:1, :] == ids) | (meta_ref[0, 1:2, :] == ids)
+    place = jnp.where(place, 1.0, 0.0).astype(jnp.bfloat16)
+    total = rows_dot(place, rows, ((0,), (0,)))
+    if adds:
+        total = total + refs[count][...].astype(jnp.float32)
+    out[...] = total.astype(out.dtype)
 
 
 def gather_tokens(ids, meta, pieces, received=(), after=(), blocks=2):
@@ -234,23 +233,19 @@
         + [part] * len(pieces)
         + [whole] * len(received)
         + [pl.BlockSpec(memory_space=pl.ANY)] * len(after),
-        out_specs=[whole, whole],
-        out_shape=[
-            jax.ShapeDtypeStruct((tokens, width), jnp.float32),
-            jax.ShapeDtypeStruct((tokens, width), jnp.bfloat16),
-        ],
+        out_specs=whole,
+        out_shape=jax.ShapeDtypeStruct((tokens, width), jnp.bfloat16),
         compiler_params=pltpu.CompilerParams(vmem_limit_bytes=VMEM),
         name="gather_tokens",
     )(ids, meta, *pieces, *received, *after)
 
 
-def expert_kernel(count, half, after, saved_ref, down_ref, gate_ref, up_ref, *refs):
+def expert_kernel(count, half, after, place_ref, saved_ref, down_ref, gate_ref, up_ref, *refs):
     pieces, refs = refs[:count], refs[count + after :]
-    outs = refs[:count]
-    hidden, gate_low, up_low = refs[count:]
+    out_ref, hidden, gate_low, up_low = refs
     step = pl.program_id(0)
     width = gate_low.shape[1]
-    size = outs[0].shape[0]
+    targets, size = out_ref.shape[:2]
 
     @pl.when(step < half)
     def _():
@@ -277,12 +272,13 @@
     @pl.when(step >= half)
     def _():
         result = rows_dot(gate_low[...], gate_ref[...], ((1,), (1,)))
-        result = (result + rows_dot(up_low[...], up_ref[...], ((1,), (1,)))).astype(jnp.bfloat16)
-        for index, out in enumerate(outs):
-            out[...] = result[index * size : (index + 1) * size]
-
-
-def expert(saved, w_down, w_gate, w_up, pieces, after=(), half=2):
+        result = result + rows_dot(up_low[...], up_ref[...], ((1,), (1,)))
+        for index in range(targets):
+            block = result[index * size : (index + 1) * size]
+            out_ref[place_ref[0] ^ index] = block.astype(jnp.bfloat16)
+
+
+def expert(place, targets, saved, w_down, w_gate, w_up, pieces, after=(), half=2):
     size, width = pieces[0].shape
     hidden = w_down.shape[0]
     count = len(pieces)
@@ -294,6 +290,7 @@
         functools.partial(expert_kernel, count, half, len(after)),
         grid=(2 * half,),
         in_specs=[
+            pl.BlockSpec(memory_space=pltpu.SMEM),
             pl.BlockSpec((rows, 2 * hidden), lambda i: (0, 0)),
             pl.BlockSpec((hidden, cols), early),
             pl.BlockSpec((cols, hidden), late),
@@ -301,8 +298,10 @@
         ]
         + [pl.BlockSpec((size, cols), early)] * count
         + [pl.BlockSpec(memory_space=pl.ANY)] * len(after),
-        out_specs=[pl.BlockSpec((size, cols), lambda i: (0, jnp.maximum(i - half, 0)))] * count,
-        out_shape=[jax.ShapeDtypeStruct((size, width), jnp.bfloat16)] * count,
+        out_specs=pl.BlockSpec(
+            (targets, rows // targets, cols), lambda i: (0, 0, jnp.maximum(i - half, 0))
+        ),
+        out_shape=jax.ShapeDtypeStruct((targets, rows // targets, width), jnp.bfloat16),
         scratch_shapes=[
             pltpu.VMEM((rows, hidden), jnp.float32),
             pltpu.VMEM((rows, hidden), jnp.bfloat16),
@@ -310,7 +309,7 @@
         ],
         compiler_params=pltpu.CompilerParams(vmem_limit_bytes=VMEM),
         name="expert_piece",
-    )(saved, w_down, w_gate, w_up, *pieces, *after)
+    )(place, saved, w_down, w_gate, w_up, *pieces, *after)
 
 
 def positions(span_ids, row_ids, span):
@@ -370,6 +369,10 @@
     )
     ids = ids.reshape(chips * 2 * padded, 2).astype(jnp.float32)
 
+    back_owner = (jnp.arange(ctx_size, dtype=jnp.int32) * exp_size + exp_index) // 2
+    back_ids = jnp.where(j_ids < capacity, back_owner[:, None] * capacity + j_ids, -1)
+    back_ids = back_ids.reshape(ctx_size * padded, 1).astype(jnp.float32)
+
     saved = gate_up_saved[0]
     if padded != capacity:
         saved = jnp.pad(saved, ((0, 0), (0, padded - capacity), (0, 0)))
@@ -379,9 +382,7 @@
     saved = jnp.take(saved, picks, axis=0, mode="clip")
     saved = saved.reshape(exp_size, ctx_size * padded, saved.shape[2])
 
-    def across(pieces, gate=()):
-        if gate:
-            pieces = lax.optimization_barrier((*pieces, *gate))[: len(pieces)]
+    def across(pieces):
         return [pieces[0]] + [swap(piece, 2 * m) for m, piece in enumerate(pieces) if m > 0]
 
     held = [packed]
@@ -406,16 +407,23 @@
         slots[s], metas[s] = build_slots(ids, capacity, held[s], other[s], chips, (*last, *needs))
         last = (slots[s][0],)
 
+    place = ctx_index.astype(jnp.int32)[None]
+
     def apply(s, needs=()):
         nonlocal last
-        rows[s] = expert(saved[s], w_down[0], w_gate[0], w_up[0], sent[s], (*last, *needs))
-        last = (rows[s][0],)
+        rows[s] = expert(
+            place, ctx_size, saved[s], w_down[0], w_gate[0], w_up[0], sent[s], (*last, *needs)
+        )
+        last = (rows[s],)
+
+    def back(s, gate=()):
+        leaving = lax.optimization_barrier((rows[s], *gate))[0] if gate else rows[s]
+        came = lax.all_to_all(leaving, "ctx", 0, 0, tiled=True)
+        results[s] = [came.reshape(ctx_size * padded, came.shape[2])]
 
     def gather(s, received=(), needs=()):
         nonlocal last
-        own, sibling = gather_tokens(ids, metas[s], results[s], received, (*last, *needs))
-        total = own + swap(sibling, 1).astype(jnp.float32)
-        total = total.astype(jnp.bfloat16)
+        total = gather_tokens(back_ids, metas[s], results[s], received, (*last, *needs))
         last = (total,)
         return total
 
@@ -437,43 +445,45 @@
         attention_parts.append(done)
 
     def send(s, gate=()):
-        sent[s] = across(slots[s], gate)
-
-    def back(s, gate=()):
-        results[s] = across(rows[s], gate)
+        pieces = list(slots[s])
+        if gate:
+            pieces = list(lax.optimization_barrier((*pieces, *gate))[: len(pieces)])
+        sent[s] = across(pieces)
 
     build(0)
-    send(0)
+    near = [m for m in range(1, chips) if m & (m - 1) == 0]
+    far = [m for m in range(1, chips) if m & (m - 1)]
+    first = {m: swap(slots[0][m], 2 * m) for m in near}
     attend(0)
-    arrive(sent[0][1:])
-    attend(1)
+    arrive([first[m] for m in near])
+    late = lax.optimization_barrier((held[1], *[slots[0][m] for m in far]))[1:]
+    first.update({m: swap(piece, 2 * m) for m, piece in zip(far, late)})
+    sent[0] = [slots[0][0]] + [first[m] for m in range(1, chips)]
     build(1)
     send(1)
-    apply(0)
-    arrive(sent[1][1:])
+    attend(1)
+    attend(2)
+    arrive([*sent[1][1:], *(first[m] for m in far)])
     build(2)
     send(2)
     apply(1)
     ring = ()
     for s in range(3, exp_size):
         arrive(sent[s - 1][1:])
-        back(s - 2, sent[s - 1][1:])
-        if s == 3:
-            attend(2)
+        back(s - 2, last)
         build(s)
-        if s == 3:
-            attend(3)
-        send(s, results[s - 2][1:])
-        total = gather(s - 2, ring)
-        ring = (turn(total),)
+        send(s)
         apply(s - 1)
-        if s == exp_size - 1:
-            back(s - 1, sent[s][1:])
-    apply(exp_size - 1, sent[exp_size - 1][1:])
-    back(exp_size - 1, results[exp_size - 2][1:])
+        ring = (turn(gather(s - 2, ring, sent[s][1:])),)
+    back(exp_size - 2, last)
+    apply(exp_size - 1)
+    apply(0)
     ring = (turn(gather(exp_size - 2, ring)),)
-    back(0, results[exp_size - 1][1:])
+    back(exp_size - 1, last)
+    attend(3)
     ring = (turn(gather(exp_size - 1, ring)),)
+    after_rings = last
+    back(0, last)
     token_out = gather(0, ring)[None]
 
     query_out = jnp.concatenate([done[0] for done in attention_parts], axis=1)
@@ -481,9 +491,17 @@
     key_part = jnp.concatenate([done[1] for done in ends], axis=1).astype(jnp.bfloat16)
     value_part = jnp.concatenate([done[2] for done in ends], axis=1).astype(jnp.bfloat16)
     part = jnp.concatenate([key_part, value_part], axis=1)
+    part = lax.optimization_barrier((part, *after_rings))[0]
     part = part.reshape(ctx_size, tokens, 2 * width_kv)
-    part = lax.all_to_all(part, "ctx", 0, 0, tiled=True).astype(jnp.float32)
-    part = jnp.sum(part, axis=0, keepdims=True).astype(jnp.bfloat16)
+    mask = 1
+    while mask < ctx_size:
+        pair = part.reshape(part.shape[0] // 2, 2, tokens, 2 * width_kv)
+        upper = (ctx_index // mask) % 2 == 1
+        mine = jnp.where(upper, pair[:, 1], pair[:, 0]).astype(jnp.float32)
+        yours = jnp.where(upper, pair[:, 0], pair[:, 1]).astype(jnp.bfloat16)
+        part = mine + swap(yours, mask).astype(jnp.float32)
+        mask *= 2
+    part = part.astype(jnp.bfloat16)
     return (query_out[None], part[..., :width_kv], part[..., width_kv:], token_out)
 
 

time: 266 us -> 249 us (0.936); the launches traced: 261 us -> 248 us
  waiting for transfers between devices: 81.6 us -> 73.4 us
  other arithmetic: 13.2 us -> 9.05 us
  Pallas kernels: 108 us -> 104 us
    ppermute x32 -> x19, waiting for transfers between devices: 58 us -> 39 us  [swap(): return lax.ppermute(value, 'ctx', [(i, i ^ mask) for i in range(count)])]
    all_to_all x1 -> x4, starting transfers between devices: 3.56 us -> 16.2 us  [back(): came = lax.all_to_all(leaving, 'ctx', 0, 0, tiled=True)]
    ppermute x6, waiting for transfers between devices: 16.7 us -> 27.5 us  [turn(): lax.ppermute(value, 'exp', [(i, (i + steps) % count) for i in range(count)])]
    ppermute x32 -> x19, starting transfers between devices: 28.3 us -> 18.8 us  [swap(): return lax.ppermute(value, 'ctx', [(i, i ^ mask) for i in range(count)])]
    convert_element_type x3 -> x4, other arithmetic: 5.7 us -> 0.21 us  [the longest x2 0.08 us: shards(): yours = jnp.where(upper, pair[:, 0], pair[:, 1]).astype(jnp.bfloat16)]
    pallas_call x4, Pallas kernels: 15 us -> 11.8 us  [gather_tokens(): pl.pallas_call(functools.partial(tokens_kernel, len(pieces), len(received...]
    broadcast_in_dim x1 -> x0, other arithmetic: 2.92 us -> none  [shards(): token_out = gather(0, ring)[None]]
    unnamed x98 -> x64, local copies, waits for them, and re-layouts: 6.26 us -> 7.5 us
  transfers between devices with their start and end apart: 40 -> 30, of which waited for: 22 -> 12; matrix products, arithmetic and copies ran while one was open for 4% -> 6% of each run, Pallas kernels for 36% -> 36%
where the time goes in v1:
time: 249 us; the launch traced here: 248 us
  Pallas kernels  104 us (42%)
  waiting for transfers between devices  73.4 us (29%)
  starting transfers between devices  45.3 us (18%)
  local copies, waits for them, and re-layouts  14.6 us (6%)
  other arithmetic  9.05 us (4%)
    pallas_call x4, Pallas kernels, expert(): pl.pallas_call(functools.partial(expert_kernel, count, half, len(after)),...  51.1 us
    ppermute x19, waiting for transfers between devices, swap(): return lax.ppermute(value, 'ctx', [(i, i ^ mask) for i in range(count)])  39 us
    ppermute x6, waiting for transfers between devices, turn(): lax.ppermute(value, 'exp', [(i, (i + steps) % count) for i in range(count)])  27.5 us
    pallas_call x4, Pallas kernels, attention(): pl.pallas_call(functools.partial(attention_kernel, after=len(after)), gri...  25.7 us
    ppermute x19, starting transfers between devices, swap(): return lax.ppermute(value, 'ctx', [(i, i ^ mask) for i in range(count)])  18.8 us
    all_to_all x4, starting transfers between devices, back(): came = lax.all_to_all(leaving, 'ctx', 0, 0, tiled=True)  16.2 us
    pallas_call x4, Pallas kernels, build_slots(): pl.pallas_call(functools.partial(slots_kernel, capacity, len(after)), gri...  13.4 us
    pallas_call x4, Pallas kernels, gather_tokens(): pl.pallas_call(functools.partial(tokens_kernel, len(pieces), len(received...  11.8 us
  transfers between devices with their start and end apart: 30, of which 12 were waited for; matrix products, arithmetic and copies ran while one was open for 6% of the time, Pallas kernels for 36%

profile of v1, /device:TPU:0, one launch (start us, length us, event | category | flops | bytes accessed | tf_op | source)
XLA Modules:
  0.0 248.0 jit_solution(9176220374876213732)
XLA Ops:
  0.7 2.5 %pack_tokens.1.own_x.own_ref = bf16[128,4224]{1,0:T(8,128)(2,1)} custom-call(bf16[128,4096]{1,0:T(8,128)(2,1)} %bitcast.121, s32[2,128]{1,0:T(2,128)} %bitcast.125, f32[2,128]{1,0:T(2,128)} %bitcast.126), custom_call_target="tpu_custom_call" | custom-call | tf_op jit(solution)/shard_map/pack_tokens/pallas_call | solution.py:124
  3.6 2.6 %collective-permute-start.1 = (bf16[128,4224]{1,0:T(8,128)(2,1)}, bf16[128,4224]{1,0:T(8,128)(2,1)}, u32[]{:S(2)}, u32[]{:S(2)}) collective-permute-start(bf16[128,4224]{1,0:T(8,128)(2,1)} %pack_tokens.1.own_x.own_ref), channel_id=1, source_target_pairs={{0,1},{1,2},{2,3},{3,0},{4,5},{5,6},{6,7},{7,4},{8,9},{9,10},{10,1... | collective-permute-start | bytes 3244040 | tf_op jit(solution)/shard_map/ppermute | solution.py:30
  7.3 3.7 %all-to-all-start = ((bf16[8,128,512]{2,1,0:T(8,128)(2,1)}), bf16[8,128,512]{2,1,0:T(8,128)(2,1)S(1)}, u32[]{:S(2)}, u32[]{:S(2)}) async-start(bf16[8,128,512]{2,1,0:T(8,128)(2,1)} %broadcast_in_dim.116), calls=%async_computation | async-start | bytes 2097152 | tf_op jit(solution)/shard_map/all_to_all | solution.py:350
  12.2 3.3 %build_slots.4 = (bf16[48,4096]{1,0:T(8,128)(2,1)}, bf16[48,4096]{1,0:T(8,128)(2,1)}, bf16[48,4096]{1,0:T(8,128)(2,1)}, bf16[48,4096]{1,0:T(8,128)(2,1)}, f32[2,4,128]{2,1,0:T(4,128)}) custom-call(f32[192,2]{1,0:T(8,128)} %select_convert_fusion.2.ids_ref, bf16[128,4224]{1,0:T(8,128)(2,1)} %pack_tokens.1.own_x.own_ref, ...), custom_call_target="tpu_custom_call" | custom-call | tf_op jit(solution)/shard_map/build_slots/pallas_call | solution.py:189
  15.5 2.0 collective-permute-start.2
  17.5 1.5 collective-permute-start.3
  20.0 6.9 %all-to-all-done = bf16[8,128,512]{2,1,0:T(8,128)(2,1)S(1)} async-done(((bf16[8,128,512]{2,1,0:T(8,128)(2,1)}), bf16[8,128,512]{2,1,0:T(8,128)(2,1)S(1)}, u32[]{:S(2)}, u32[]{:S(2)}) %all-to-all-start) | async-done | bytes 1048608 | tf_op jit(solution)/shard_map/all_to_all | solution.py:350
  28.1 6.5 %attention_core.4 = (bf16[128,1024]{1,0:T(8,128)(2,1)}, f32[1024,128]{1,0:T(8,128)}, f32[1024,128]{1,0:T(8,128)}) custom-call(f32[1024,128]{1,0:T(8,128)} %compare_select_fusion.bias_ref, bf16[128,4096]{1,0:T(8,128)(2,1)} %bitcast.103, bf16[128,4096]{1,0:T(8,128)(2,1)} %bitcast.107, bf16[1024,512]{1,0:T(8,128)(2,1)} %bitcast.95, bf16[1024,512]{1,0:T(8,128)(2,1)} %bitcast.96, ...), custom_call_target="tpu_custom_call" | custom-call | tf_op jit(solution)/shard_map/attention_core/pallas_call | solution.py:94
  34.6 1.8 collective-permute-start.5
  38.5 3.3 %build_slots.5 = (bf16[48,4096]{1,0:T(8,128)(2,1)}, bf16[48,4096]{1,0:T(8,128)(2,1)}, bf16[48,4096]{1,0:T(8,128)(2,1)}, bf16[48,4096]{1,0:T(8,128)(2,1)}, f32[2,4,128]{2,1,0:T(4,128)}) custom-call(f32[192,2]{1,0:T(8,128)} %select_convert_fusion.2.ids_ref, bf16[128,4224]{1,0:T(8,128)(2,1)} %collective-permute-done.1.own_x.own_ref, ...), custom_call_target="tpu_custom_call" | custom-call | tf_op jit(solution)/shard_map/build_slots/pallas_call | solution.py:189
  42.9 1.3 collective-permute-start.7
  45.3 6.4 %attention_core.5 = (bf16[128,1024]{1,0:T(8,128)(2,1)}, f32[1024,128]{1,0:T(8,128)}, f32[1024,128]{1,0:T(8,128)}) custom-call(f32[1024,128]{1,0:T(8,128)} %compare_select_fusion.bias_ref, bf16[128,4096]{1,0:T(8,128)(2,1)} %bitcast.104, bf16[128,4096]{1,0:T(8,128)(2,1)} %bitcast.108, bf16[1024,512]{1,0:T(8,128)(2,1)} %bitcast.97, bf16[1024,512]{1,0:T(8,128)(2,1)} %bitcast.98, ...), custom_call_target="tpu_custom_call" | custom-call | tf_op jit(solution)/shard_map/attention_core/pallas_call | solution.py:94
  51.7 6.4 %attention_core.6 = (bf16[128,1024]{1,0:T(8,128)(2,1)}, f32[1024,128]{1,0:T(8,128)}, f32[1024,128]{1,0:T(8,128)}) custom-call(f32[1024,128]{1,0:T(8,128)} %compare_select_fusion.bias_ref, bf16[128,4096]{1,0:T(8,128)(2,1)} %bitcast.105, bf16[128,4096]{1,0:T(8,128)(2,1)} %bitcast.109, bf16[1024,512]{1,0:T(8,128)(2,1)} %bitcast.99, ...), custom_call_target="tpu_custom_call" | custom-call | tf_op jit(solution)/shard_map/attention_core/pallas_call | solution.py:94
  58.1 4.8 %collective-permute-done.5.own_x.own_ref = bf16[128,4224]{1,0:T(8,128)(2,1)S(1)} collective-permute-done((bf16[128,4224]{1,0:T(8,128)(2,1)}, bf16[128,4224]{1,0:T(8,128)(2,1)S(1)}, u32[]{:S(2)}, u32[]{:S(2)}) %collective-permute-start.5) | collective-permute-done | bytes 1081376 | tf_op jit(solution)/shard_map/ppermute | solution.py:30
  62.9 2.3 collective-permute-done.8.refs_3_
  65.3 1.8 collective-permute-start.14
  67.3 2.1 gather_fusion
  69.4 3.4 %build_slots.6 = (bf16[48,4096]{1,0:T(8,128)(2,1)}, bf16[48,4096]{1,0:T(8,128)(2,1)}, bf16[48,4096]{1,0:T(8,128)(2,1)}, bf16[48,4096]{1,0:T(8,128)(2,1)}, f32[2,4,128]{2,1,0:T(4,128)}) custom-call(f32[192,2]{1,0:T(8,128)} %select_convert_fusion.2.ids_ref, bf16[128,4224]{1,0:T(8,128)(2,1)} %copy-done.6, ...), custom_call_target="tpu_custom_call" | custom-call | tf_op jit(solution)/shard_map/build_slots/pallas_call | solution.py:189
  74.3 2.0 collective-permute-start.13
  76.3 1.5 fusion.18
  77.8 12.9 %expert_piece.4.refs_0_ = bf16[8,24,4096]{2,1,0:T(8,128)(2,1)} custom-call(s32[1]{0:T(128)} %bitcast.12.place_ref, bf16[192,1536]{1,0:T(8,128)(2,1)} %bitcast.119, bf16[768,4096]{1,0:T(8,128)(2,1)} %bitcast.83, bf16[4096,768]{1,0:T(8,128)(2,1)} %bitcast.87, bf16[4096,768]{1,0:T(8,128)(2,1)} %bitcast.91, bf16[48,4096]{1,0:T(8,128)(2,1)} %get-tuple-element.56.refs_0_, ...), custom_call_target="tpu_custom_call" | custom-call | tf_op jit(solution)/shard_map/expert_piece/pallas_call | solution.py:289
  90.7 2.8 %collective-permute-done.14.own_x.own_ref = bf16[128,4224]{1,0:T(8,128)(2,1)} collective-permute-done((bf16[128,4224]{1,0:T(8,128)(2,1)S(1)}, bf16[128,4224]{1,0:T(8,128)(2,1)}, u32[]{:S(2)}, u32[]{:S(2)}) %collective-permute-start.14) | collective-permute-done | bytes 1081376 | tf_op jit(solution)/shard_map/ppermute | solution.py:30
  95.7 3.6 %all-to-all-start.1 = ((bf16[8,24,4096]{2,1,0:T(8,128)(2,1)}), bf16[8,24,4096]{2,1,0:T(8,128)(2,1)S(1)}, u32[]{:S(2)}, u32[]{:S(2)}) async-start(bf16[8,24,4096]{2,1,0:T(8,128)(2,1)} %expert_piece.4.refs_0_), calls=%async_computation.1 | async-start | bytes 3145728 | tf_op jit(solution)/shard_map/all_to_all | solution.py:421
  100.3 3.4 %build_slots.7 = (bf16[48,4096]{1,0:T(8,128)(2,1)}, bf16[48,4096]{1,0:T(8,128)(2,1)}, bf16[48,4096]{1,0:T(8,128)(2,1)}, bf16[48,4096]{1,0:T(8,128)(2,1)}, f32[2,4,128]{2,1,0:T(4,128)}) custom-call(f32[192,2]{1,0:T(8,128)} %select_convert_fusion.2.ids_ref, bf16[128,4224]{1,0:T(8,128)(2,1)} %collective-permute-done.14.own_x.own_ref, ...), custom_call_target="tpu_custom_call" | custom-call | tf_op jit(solution)/shard_map/build_slots/pallas_call | solution.py:189
  103.6 1.9 collective-permute-start.16
  105.6 1.5 collective-permute-start.17
  108.0 12.8 %expert_piece.5.refs_1_ = bf16[8,24,4096]{2,1,0:T(8,128)(2,1)} custom-call(s32[1]{0:T(128)} %bitcast.12.place_ref, bf16[192,1536]{1,0:T(8,128)(2,1)} %bitcast.118, bf16[768,4096]{1,0:T(8,128)(2,1)} %bitcast.84, bf16[4096,768]{1,0:T(8,128)(2,1)} %bitcast.88, bf16[4096,768]{1,0:T(8,128)(2,1)} %bitcast.92, bf16[48,4096]{1,0:T(8,128)(2,1)} %get-tuple-element.69.refs_4_.refs_0_, ...), custom_call_target="tpu_custom_call" | custom-call | tf_op jit(solution)/shard_map/expert_piece/pallas_call | solution.py:289
  120.8 7.5 %collective-permute-done.16.refs_2_.refs_1_ = bf16[48,4096]{1,0:T(8,128)(2,1)S(1)} collective-permute-done((bf16[48,4096]{1,0:T(8,128)(2,1)}, bf16[48,4096]{1,0:T(8,128)(2,1)S(1)}, u32[]{:S(2)}, u32[]{:S(2)}) %collective-permute-start.16) | collective-permute-done | bytes 393248 | tf_op jit(solution)/shard_map/ppermute | solution.py:25
  128.3 8.9 %collective-permute-done.18.refs_4_.refs_3_ = bf16[48,4096]{1,0:T(8,128)(2,1)S(1)} collective-permute-done((bf16[48,4096]{1,0:T(8,128)(2,1)}, bf16[48,4096]{1,0:T(8,128)(2,1)S(1)}, u32[]{:S(2)}, u32[]{:S(2)}) %collective-permute-start.18) | collective-permute-done | bytes 393248 | tf_op jit(solution)/shard_map/ppermute | solution.py:25
  137.9 2.8 %gather_tokens.4.refs_4_ = bf16[128,4096]{1,0:T(8,128)(2,1)} custom-call(f32[192,1]{1,0:T(8,128)} %convert_element_type.62.ids_ref, f32[2,4,128]{2,1,0:T(4,128)} %get-tuple-element.76.meta_ref, bf16[192,4096]{1,0:T(8,128)(2,1)} %bitcast.115, bf16[8,24,4096]{2,1,0:T(8,128)(2,1)} %expert_piece.5.refs_1_, bf16[48,4096]{1,0:T(8,128)(2,1)} %copy-done.12, ...), custom_call_target="tpu_custom_call" | custom-call | tf_op jit(solution)/shard_map/gather_tokens/pallas_call | solution.py:226
  140.7 3.7 %all-to-all-start.2 = ((bf16[8,24,4096]{2,1,0:T(8,128)(2,1)}), bf16[8,24,4096]{2,1,0:T(8,128)(2,1)S(1)}, u32[]{:S(2)}, u32[]{:S(2)}) async-start(bf16[8,24,4096]{2,1,0:T(8,128)(2,1)} %expert_piece.5.refs_1_), calls=%async_computation.2 | async-start | bytes 3145728 | tf_op jit(solution)/shard_map/all_to_all | solution.py:421
  144.8 12.7 %expert_piece.6.refs_4_ = bf16[8,24,4096]{2,1,0:T(8,128)(2,1)} custom-call(s32[1]{0:T(128)} %bitcast.12.place_ref, bf16[192,1536]{1,0:T(8,128)(2,1)} %bitcast.117, bf16[768,4096]{1,0:T(8,128)(2,1)} %bitcast.85, bf16[4096,768]{1,0:T(8,128)(2,1)} %bitcast.89, bf16[4096,768]{1,0:T(8,128)(2,1)} %bitcast.93, bf16[48,4096]{1,0:T(8,128)(2,1)} %get-tuple-element.75.refs_4_.refs_0_, ...), custom_call_target="tpu_custom_call" | custom-call | tf_op jit(solution)/shard_map/expert_piece/pallas_call | solution.py:289
  157.5 12.8 %expert_piece.7.refs_2_ = bf16[8,24,4096]{2,1,0:T(8,128)(2,1)} custom-call(s32[1]{0:T(128)} %bitcast.12.place_ref, bf16[192,1536]{1,0:T(8,128)(2,1)} %bitcast.120, bf16[768,4096]{1,0:T(8,128)(2,1)} %bitcast.86, bf16[4096,768]{1,0:T(8,128)(2,1)} %bitcast.90, bf16[4096,768]{1,0:T(8,128)(2,1)} %bitcast.94, bf16[48,4096]{1,0:T(8,128)(2,1)} %get-tuple-element.48.refs_0_, ...), custom_call_target="tpu_custom_call" | custom-call | tf_op jit(solution)/shard_map/expert_piece/pallas_call | solution.py:289
  170.3 1.5 collective-permute-done.19.refs_1_
  173.0 3.0 %gather_tokens.5.refs_0_ = bf16[128,4096]{1,0:T(8,128)(2,1)} custom-call(f32[192,1]{1,0:T(8,128)} %convert_element_type.62.ids_ref, f32[2,4,128]{2,1,0:T(4,128)} %get-tuple-element.68.meta_ref, bf16[192,4096]{1,0:T(8,128)(2,1)} %bitcast.116, bf16[128,4096]{1,0:T(8,128)(2,1)} %collective-permute-done.19.refs_1_, bf16[8,24,4096]{2,1,0:T(8,128)(2,1)} %expert_piece.7.refs_2_), custom_call_target="tpu_custom_call" | custom-call | tf_op jit(solution)/shard_map/gather_tokens/pallas_call | solution.py:226
  176.0 4.5 %all-to-all-start.3 = ((bf16[8,24,4096]{2,1,0:T(8,128)(2,1)}), bf16[8,24,4096]{2,1,0:T(8,128)(2,1)}, u32[]{:S(2)}, u32[]{:S(2)}) async-start(bf16[8,24,4096]{2,1,0:T(8,128)(2,1)} %expert_piece.6.refs_4_), calls=%async_computation.3 | async-start | bytes 3145728 | tf_op jit(solution)/shard_map/all_to_all | solution.py:421
  180.6 6.4 %attention_core.7 = (bf16[128,1024]{1,0:T(8,128)(2,1)}, f32[1024,128]{1,0:T(8,128)}, f32[1024,128]{1,0:T(8,128)}) custom-call(f32[1024,128]{1,0:T(8,128)} %compare_select_fusion.bias_ref, bf16[128,4096]{1,0:T(8,128)(2,1)} %bitcast.106, bf16[128,4096]{1,0:T(8,128)(2,1)} %bitcast.110, bf16[1024,512]{1,0:T(8,128)(2,1)} %bitcast.101, ...), custom_call_target="tpu_custom_call" | custom-call | tf_op jit(solution)/shard_map/attention_core/pallas_call | solution.py:94
  189.3 18.4 %collective-permute-done.20.refs_1_ = bf16[128,4096]{1,0:T(8,128)(2,1)S(1)} collective-permute-done((bf16[128,4096]{1,0:T(8,128)(2,1)S(1)}, bf16[128,4096]{1,0:T(8,128)(2,1)S(1)}, u32[]{:S(2)}, u32[]{:S(2)}) %collective-permute-start.20) | collective-permute-done | bytes 1048608 | tf_op jit(solution)/shard_map/ppermute | solution.py:30
  208.7 3.0 %gather_tokens.6.refs_2_ = bf16[128,4096]{1,0:T(8,128)(2,1)} custom-call(f32[192,1]{1,0:T(8,128)} %convert_element_type.62.ids_ref, f32[2,4,128]{2,1,0:T(4,128)} %get-tuple-element.87.meta_ref, bf16[192,4096]{1,0:T(8,128)(2,1)} %bitcast.24.refs_0_, bf16[128,4096]{1,0:T(8,128)(2,1)} %copy-done.15, bf16[128,1024]{1,0:T(8,128)(2,1)} %get-tuple-element.82.refs_2_), custom_call_target="tpu_custom_call" | custom-call | tf_op jit(solution)/shard_map/gather_tokens/pallas_call | solution.py:226
  211.8 2.0 collective-permute-done.21
  213.8 1.2 convert_add_fusion
  215.1 1.7 collective-permute-start.22
  216.9 4.4 %all-to-all-start.4 = ((bf16[8,24,4096]{2,1,0:T(8,128)(2,1)}), bf16[8,24,4096]{2,1,0:T(8,128)(2,1)}, u32[]{:S(2)}, u32[]{:S(2)}) async-start(bf16[8,24,4096]{2,1,0:T(8,128)(2,1)} %expert_piece.7.refs_2_), calls=%async_computation.4 | async-start | bytes 3145728 | tf_op jit(solution)/shard_map/all_to_all | solution.py:421
  221.4 2.3 collective-permute-done.22
  224.7 1.8 collective-permute-start.23
  226.5 2.0 maximum_bitcast_fusion
  228.5 15.6 %collective-permute-done.23 = bf16[1,128,512]{2,1,0:T(8,128)(2,1)S(1)} collective-permute-done((bf16[1,128,512]{2,1,0:T(8,128)(2,1)S(1)}, bf16[1,128,512]{2,1,0:T(8,128)(2,1)S(1)}, u32[]{:S(2)}, u32[]{:S(2)}) %collective-permute-start.23) | collective-permute-done | bytes 131104 | tf_op jit(solution)/shard_map/ppermute | solution.py:25
  244.9 3.1 %gather_tokens.7 = bf16[128,4096]{1,0:T(8,128)(2,1)} custom-call(f32[192,1]{1,0:T(8,128)} %convert_element_type.62.ids_ref, f32[2,4,128]{2,1,0:T(4,128)} %get-tuple-element.90.meta_ref, bf16[192,4096]{1,0:T(8,128)(2,1)} %bitcast.37.refs_0_, bf16[128,4096]{1,0:T(8,128)(2,1)} %collective-permute-done.24.refs_1_, bf16[128,4096]{1,0:T(8,128)(2,1)} %gather_tokens.6.refs_2_), custom_call_target="tpu_custom_call" | custom-call | tf_op jit(solution)/shard_map/gather_tokens/pallas_call | solution.py:226
  (132 shorter events, 22.8 us)
Async XLA Ops:
  0.6 66.6 %copy-start = (bf16[1,32,24,1536]{3,2,1,0:T(8,128)(2,1)S(1)}, bf16[1,32,24,1536]{3,2,1,0:T(8,128)(2,1)}, u32[]{:S(2)}) copy-start(bf16[1,32,24,1536]{3,2,1,0:T(8,128)(2,1)} %param.23) | copy-start | bytes 7077892
  0.6 5.5 %copy-start.28 = (bf16[1,128,256]{2,1,0:T(8,128)(2,1)S(1)}, bf16[1,128,256]{2,1,0:T(8,128)(2,1)}, u32[]{:S(2)}) copy-start(bf16[1,128,256]{2,1,0:T(8,128)(2,1)} %param.14) | copy-start | bytes 196612
  0.7 5.5 %copy-start.29 = (bf16[1,128,256]{2,1,0:T(8,128)(2,1)S(1)}, bf16[1,128,256]{2,1,0:T(8,128)(2,1)}, u32[]{:S(2)}) copy-start(bf16[1,128,256]{2,1,0:T(8,128)(2,1)} %param.13) | copy-start | bytes 196612
  3.2 8.8 %copy-start.30 = (s32[1,16]{1,0:T(1,128)S(1)}, s32[1,16]{1,0:T(1,128)}, u32[]{:S(2)}) copy-start(s32[1,16]{1,0:T(1,128)} %param.16) | copy-start | bytes 196
  3.2 9.0 %collective-permute-start = (bf16[128,4224]{1,0:T(8,128)(2,1)}, bf16[128,4224]{1,0:T(8,128)(2,1)}, u32[]{:S(2)}, u32[]{:S(2)}) collective-permute-start(bf16[128,4224]{1,0:T(8,128)(2,1)} %pack_tokens.1.own_x.own_ref), channel_id=1, source_target_pairs={{0,4},{4,0},{8,12},{12,8},{16,20},{20,16},{24,28},{28,24},{1,5},{5... | collective-permute-start | bytes 3244040 | tf_op jit(solution)/shard_map/ppermute | solution.py:25
  3.6 30.9 %collective-permute-start.1 = (bf16[128,4224]{1,0:T(8,128)(2,1)}, bf16[128,4224]{1,0:T(8,128)(2,1)}, u32[]{:S(2)}, u32[]{:S(2)}) collective-permute-start(bf16[128,4224]{1,0:T(8,128)(2,1)} %pack_tokens.1.own_x.own_ref), channel_id=1, source_target_pairs={{0,1},{1,2},{2,3},{3,0},{4,5},{5,6},{6,7},{7,4},{8,9},{9,10},{10,1... | collective-permute-start | bytes 3244040 | tf_op jit(solution)/shard_map/ppermute | solution.py:30
  7.3 19.7 %all-to-all-start = ((bf16[8,128,512]{2,1,0:T(8,128)(2,1)}), bf16[8,128,512]{2,1,0:T(8,128)(2,1)S(1)}, u32[]{:S(2)}, u32[]{:S(2)}) async-start(bf16[8,128,512]{2,1,0:T(8,128)(2,1)} %broadcast_in_dim.116), calls=%async_computation | async-start | bytes 2097152 | tf_op jit(solution)/shard_map/all_to_all | solution.py:350
  15.5 19.0 %collective-permute-start.2 = (bf16[48,4096]{1,0:T(8,128)(2,1)}, bf16[48,4096]{1,0:T(8,128)(2,1)}, u32[]{:S(2)}, u32[]{:S(2)}) collective-permute-start(bf16[48,4096]{1,0:T(8,128)(2,1)} %get-tuple-element.52), channel_id=1, source_target_pairs={{0,8},{4,12},{8,0},{12,4},{16,24},{20,28},{24,16},{28,20},{1,9},{5... | collective-permute-start | bytes 1179656 | tf_op jit(solution)/shard_map/ppermute | solution.py:25
  17.5 17.0 %collective-permute-start.3 = (bf16[48,4096]{1,0:T(8,128)(2,1)}, bf16[48,4096]{1,0:T(8,128)(2,1)}, u32[]{:S(2)}, u32[]{:S(2)}) collective-permute-start(bf16[48,4096]{1,0:T(8,128)(2,1)} %get-tuple-element.53), channel_id=1, source_target_pairs={{0,16},{4,20},{8,24},{12,28},{16,0},{20,4},{24,8},{28,12},{1,17},{... | collective-permute-start | bytes 1179656 | tf_op jit(solution)/shard_map/ppermute | solution.py:25
  28.1 8.4 %copy-start.31 = (bf16[48,4096]{1,0:T(8,128)(2,1)S(1)}, bf16[48,4096]{1,0:T(8,128)(2,1)}, u32[]{:S(2)}) copy-start(bf16[48,4096]{1,0:T(8,128)(2,1)} %get-tuple-element.65) | copy-start | bytes 1179652
  34.5 3.0 %collective-permute-start.4 = (bf16[128,4224]{1,0:T(8,128)(2,1)}, bf16[128,4224]{1,0:T(8,128)(2,1)S(1)}, u32[]{:S(2)}, u32[]{:S(2)}) collective-permute-start(bf16[128,4224]{1,0:T(8,128)(2,1)} %collective-permute-done.1.own_x.own_ref), channel_id=1, source_target_pairs={{0,4},{4,0},{8,12},{12,8},{16,20},{20,16},{24,28},{28,24},{1,5},{5... | collective-permute-start | bytes 3244040 | tf_op jit(solution)/shard_map/ppermute | solution.py:25
  34.6 28.3 %collective-permute-start.5 = (bf16[128,4224]{1,0:T(8,128)(2,1)}, bf16[128,4224]{1,0:T(8,128)(2,1)S(1)}, u32[]{:S(2)}, u32[]{:S(2)}) collective-permute-start(bf16[128,4224]{1,0:T(8,128)(2,1)} %collective-permute-done.1.own_x.own_ref), channel_id=1, source_target_pairs={{0,1},{1,2},{2,3},{3,0},{4,5},{5,6},{6,7},{7,4},{8,9},{9,10},{10,1... | collective-permute-start | bytes 3244040 | tf_op jit(solution)/shard_map/ppermute | solution.py:30
  36.4 21.7 %collective-permute-start.9 = (bf16[48,4096]{1,0:T(8,128)(2,1)S(1)}, bf16[48,4096]{1,0:T(8,128)(2,1)S(1)}, u32[]{:S(2)}, u32[]{:S(2)}) collective-permute-start(bf16[48,4096]{1,0:T(8,128)(2,1)S(1)} %copy-done.31), channel_id=1, source_target_pairs={{0,24},{4,28},{8,16},{12,20},{16,8},{20,12},{24,0},{28,4},{1,25},{... | collective-permute-start | bytes 1179656 | tf_op jit(solution)/shard_map/ppermute | solution.py:25
  41.8 21.1 %collective-permute-start.6 = (bf16[48,4096]{1,0:T(8,128)(2,1)}, bf16[48,4096]{1,0:T(8,128)(2,1)S(1)}, u32[]{:S(2)}, u32[]{:S(2)}) collective-permute-start(bf16[48,4096]{1,0:T(8,128)(2,1)} %get-tuple-element.61), channel_id=1, source_target_pairs={{0,8},{4,12},{8,0},{12,4},{16,24},{20,28},{24,16},{28,20},{1,9},{5... | collective-permute-start | bytes 1179656 | tf_op jit(solution)/shard_map/ppermute | solution.py:25
  42.9 20.0 %collective-permute-start.7 = (bf16[48,4096]{1,0:T(8,128)(2,1)}, bf16[48,4096]{1,0:T(8,128)(2,1)S(1)}, u32[]{:S(2)}, u32[]{:S(2)}) collective-permute-start(bf16[48,4096]{1,0:T(8,128)(2,1)} %get-tuple-element.62), channel_id=1, source_target_pairs={{0,16},{4,20},{8,24},{12,28},{16,0},{20,4},{24,8},{28,12},{1,17},{... | collective-permute-start | bytes 1179656 | tf_op jit(solution)/shard_map/ppermute | solution.py:25
  44.2 21.0 %collective-permute-start.8 = (bf16[48,4096]{1,0:T(8,128)(2,1)}, bf16[48,4096]{1,0:T(8,128)(2,1)S(1)}, u32[]{:S(2)}, u32[]{:S(2)}) collective-permute-start(bf16[48,4096]{1,0:T(8,128)(2,1)} %get-tuple-element.63), channel_id=1, source_target_pairs={{0,24},{4,28},{8,16},{12,20},{16,8},{20,12},{24,0},{28,4},{1,25},{... | collective-permute-start | bytes 1179656 | tf_op jit(solution)/shard_map/ppermute | solution.py:25
  58.1 9.0 %copy-start.27 = (bf16[48,4096]{1,0:T(8,128)(2,1)}, bf16[48,4096]{1,0:T(8,128)(2,1)S(1)}, u32[]{:S(2)}) copy-start(bf16[48,4096]{1,0:T(8,128)(2,1)S(1)} %collective-permute-done.9.refs_3_) | copy-start | bytes 1179652
  62.9 6.5 %copy-start.6 = (bf16[128,4224]{1,0:T(8,128)(2,1)}, bf16[128,4224]{1,0:T(8,128)(2,1)S(1)}, u32[]{:S(2)}) copy-start(bf16[128,4224]{1,0:T(8,128)(2,1)S(1)} %collective-permute-done.5.own_x.own_ref) | copy-start | bytes 3244036
  65.2 4.2 %collective-permute-start.10 = (bf16[128,4224]{1,0:T(8,128)(2,1)S(1)}, bf16[128,4224]{1,0:T(8,128)(2,1)}, u32[]{:S(2)}, u32[]{:S(2)}) collective-permute-start(bf16[128,4224]{1,0:T(8,128)(2,1)S(1)} %collective-permute-done.5.own_x.own_ref), channel_id=1, source_target_pairs={{0,4},{4,0},{8,12},{12,8},{16,20},{20,16},{24,28},{28,24},{1,5},{5... | collective-permute-start | bytes 3244040 | tf_op jit(solution)/shard_map/ppermute | solution.py:25
  65.3 28.2 %collective-permute-start.14 = (bf16[128,4224]{1,0:T(8,128)(2,1)S(1)}, bf16[128,4224]{1,0:T(8,128)(2,1)}, u32[]{:S(2)}, u32[]{:S(2)}) collective-permute-start(bf16[128,4224]{1,0:T(8,128)(2,1)S(1)} %collective-permute-done.5.own_x.own_ref), channel_id=1, source_target_pairs={{0,1},{1,2},{2,3},{3,0},{4,5},{5,6},{6,7},{7,4},{8,9},{9,10},{10,1... | collective-permute-start | bytes 3244040 | tf_op jit(solution)/shard_map/ppermute | solution.py:30
  69.4 7.0 %copy-start.3 = (bf16[32,24,1536]{2,1,0:T(8,128)(2,1)S(1)}, bf16[32,24,1536]{2,1,0:T(8,128)(2,1)}, u32[]{:S(2)}) copy-start(bf16[32,24,1536]{2,1,0:T(8,128)(2,1)} %gather_fusion) | copy-start | bytes 7077892
  72.8 20.6 %collective-permute-start.11 = (bf16[48,4096]{1,0:T(8,128)(2,1)}, bf16[48,4096]{1,0:T(8,128)(2,1)S(1)}, u32[]{:S(2)}, u32[]{:S(2)}) collective-permute-start(bf16[48,4096]{1,0:T(8,128)(2,1)} %get-tuple-element.70), channel_id=1, source_target_pairs={{0,8},{4,12},{8,0},{12,4},{16,24},{20,28},{24,16},{28,20},{1,9},{5... | collective-permute-start | bytes 1179656 | tf_op jit(solution)/shard_map/ppermute | solution.py:25
  73.7 19.7 %collective-permute-start.12 = (bf16[48,4096]{1,0:T(8,128)(2,1)}, bf16[48,4096]{1,0:T(8,128)(2,1)S(1)}, u32[]{:S(2)}, u32[]{:S(2)}) collective-permute-start(bf16[48,4096]{1,0:T(8,128)(2,1)} %get-tuple-element.71), channel_id=1, source_target_pairs={{0,16},{4,20},{8,24},{12,28},{16,0},{20,4},{24,8},{28,12},{1,17},{... | collective-permute-start | bytes 1179656 | tf_op jit(solution)/shard_map/ppermute | solution.py:25
  74.3 19.8 %collective-permute-start.13 = (bf16[48,4096]{1,0:T(8,128)(2,1)}, bf16[48,4096]{1,0:T(8,128)(2,1)S(1)}, u32[]{:S(2)}, u32[]{:S(2)}) collective-permute-start(bf16[48,4096]{1,0:T(8,128)(2,1)} %get-tuple-element.72), channel_id=1, source_target_pairs={{0,24},{4,28},{8,16},{12,20},{16,8},{20,12},{24,0},{28,4},{1,25},{... | collective-permute-start | bytes 1179656 | tf_op jit(solution)/shard_map/ppermute | solution.py:25
  95.7 3.6 %collective-permute-start.15 = (bf16[128,4224]{1,0:T(8,128)(2,1)}, bf16[128,4224]{1,0:T(8,128)(2,1)S(1)}, u32[]{:S(2)}, u32[]{:S(2)}) collective-permute-start(bf16[128,4224]{1,0:T(8,128)(2,1)} %collective-permute-done.14.own_x.own_ref), channel_id=1, source_target_pairs={{0,4},{4,0},{8,12},{12,8},{16,20},{20,16},{24,28},{28,24},{1,5},{5... | collective-permute-start | bytes 3244040 | tf_op jit(solution)/shard_map/ppermute | solution.py:25
  95.7 25.1 %all-to-all-start.1 = ((bf16[8,24,4096]{2,1,0:T(8,128)(2,1)}), bf16[8,24,4096]{2,1,0:T(8,128)(2,1)S(1)}, u32[]{:S(2)}, u32[]{:S(2)}) async-start(bf16[8,24,4096]{2,1,0:T(8,128)(2,1)} %expert_piece.4.refs_0_), calls=%async_computation.1 | async-start | bytes 3145728 | tf_op jit(solution)/shard_map/all_to_all | solution.py:421
  103.6 24.6 %collective-permute-start.16 = (bf16[48,4096]{1,0:T(8,128)(2,1)}, bf16[48,4096]{1,0:T(8,128)(2,1)S(1)}, u32[]{:S(2)}, u32[]{:S(2)}) collective-permute-start(bf16[48,4096]{1,0:T(8,128)(2,1)} %get-tuple-element.78), channel_id=1, source_target_pairs={{0,8},{4,12},{8,0},{12,4},{16,24},{20,28},{24,16},{28,20},{1,9},{5... | collective-permute-start | bytes 1179656 | tf_op jit(solution)/shard_map/ppermute | solution.py:25
  105.6 22.7 %collective-permute-start.17 = (bf16[48,4096]{1,0:T(8,128)(2,1)}, bf16[48,4096]{1,0:T(8,128)(2,1)S(1)}, u32[]{:S(2)}, u32[]{:S(2)}) collective-permute-start(bf16[48,4096]{1,0:T(8,128)(2,1)} %get-tuple-element.79), channel_id=1, source_target_pairs={{0,16},{4,20},{8,24},{12,28},{16,0},{20,4},{24,8},{28,12},{1,17},{... | collective-permute-start | bytes 1179656 | tf_op jit(solution)/shard_map/ppermute | solution.py:25
  107.0 30.1 %collective-permute-start.18 = (bf16[48,4096]{1,0:T(8,128)(2,1)}, bf16[48,4096]{1,0:T(8,128)(2,1)S(1)}, u32[]{:S(2)}, u32[]{:S(2)}) collective-permute-start(bf16[48,4096]{1,0:T(8,128)(2,1)} %get-tuple-element.80), channel_id=1, source_target_pairs={{0,24},{4,28},{8,16},{12,20},{16,8},{20,12},{24,0},{28,4},{1,25},{... | collective-permute-start | bytes 1179656 | tf_op jit(solution)/shard_map/ppermute | solution.py:25
  120.8 16.4 %copy-start.4 = (bf16[8,24,4096]{2,1,0:T(8,128)(2,1)}, bf16[8,24,4096]{2,1,0:T(8,128)(2,1)S(1)}, u32[]{:S(2)}) copy-start(bf16[8,24,4096]{2,1,0:T(8,128)(2,1)S(1)} %all-to-all-done.1) | copy-start | bytes 4718596
  128.3 8.9 %copy-start.12 = (bf16[48,4096]{1,0:T(8,128)(2,1)}, bf16[48,4096]{1,0:T(8,128)(2,1)S(1)}, u32[]{:S(2)}) copy-start(bf16[48,4096]{1,0:T(8,128)(2,1)S(1)} %collective-permute-done.16.refs_2_.refs_1_) | copy-start | bytes 1179652
  128.3 8.9 %copy-start.13 = (bf16[48,4096]{1,0:T(8,128)(2,1)}, bf16[48,4096]{1,0:T(8,128)(2,1)S(1)}, u32[]{:S(2)}) copy-start(bf16[48,4096]{1,0:T(8,128)(2,1)S(1)} %collective-permute-done.17.refs_3_.refs_2_) | copy-start | bytes 1179652
  140.7 31.1 %all-to-all-start.2 = ((bf16[8,24,4096]{2,1,0:T(8,128)(2,1)}), bf16[8,24,4096]{2,1,0:T(8,128)(2,1)S(1)}, u32[]{:S(2)}, u32[]{:S(2)}) async-start(bf16[8,24,4096]{2,1,0:T(8,128)(2,1)} %expert_piece.5.refs_1_), calls=%async_computation.2 | async-start | bytes 3145728 | tf_op jit(solution)/shard_map/all_to_all | solution.py:421
  144.4 27.4 %collective-permute-start.19 = (bf16[128,4096]{1,0:T(8,128)(2,1)S(1)}, bf16[128,4096]{1,0:T(8,128)(2,1)}, u32[]{:S(2)}, u32[]{:S(2)}) collective-permute-start(bf16[128,4096]{1,0:T(8,128)(2,1)S(1)} %copy-done.10), channel_id=1, source_target_pairs={{0,1},{1,2},{2,3},{3,0},{4,5},{5,6},{6,7},{7,4},{8,9},{9,10},{10,1... | collective-permute-start | bytes 3145736 | tf_op jit(solution)/shard_map/ppermute | solution.py:30
  176.0 4.5 %copy-start.11 = (bf16[128,4096]{1,0:T(8,128)(2,1)S(1)}, bf16[128,4096]{1,0:T(8,128)(2,1)}, u32[]{:S(2)}) copy-start(bf16[128,4096]{1,0:T(8,128)(2,1)} %gather_tokens.5.refs_0_) | copy-start | bytes 3145732
  176.0 4.6 %copy-start.20 = (f32[1024,128]{1,0:T(8,128)S(1)}, f32[1024,128]{1,0:T(8,128)}, u32[]{:S(2)}) copy-start(f32[1024,128]{1,0:T(8,128)} %get-tuple-element.85) | copy-start | bytes 1572868
  176.0 4.6 %copy-start.19 = (f32[1024,128]{1,0:T(8,128)S(1)}, f32[1024,128]{1,0:T(8,128)}, u32[]{:S(2)}) copy-start(f32[1024,128]{1,0:T(8,128)} %get-tuple-element.83) | copy-start | bytes 1572868
  176.0 31.7 %all-to-all-start.3 = ((bf16[8,24,4096]{2,1,0:T(8,128)(2,1)}), bf16[8,24,4096]{2,1,0:T(8,128)(2,1)}, u32[]{:S(2)}, u32[]{:S(2)}) async-start(bf16[8,24,4096]{2,1,0:T(8,128)(2,1)} %expert_piece.6.refs_4_), calls=%async_computation.3 | async-start | bytes 3145728 | tf_op jit(solution)/shard_map/all_to_all | solution.py:421
  180.5 27.2 %collective-permute-start.20 = (bf16[128,4096]{1,0:T(8,128)(2,1)S(1)}, bf16[128,4096]{1,0:T(8,128)(2,1)S(1)}, u32[]{:S(2)}, u32[]{:S(2)}) collective-permute-start(bf16[128,4096]{1,0:T(8,128)(2,1)S(1)} %copy-done.11), channel_id=1, source_target_pairs={{0,1},{1,2},{2,3},{3,0},{4,5},{5,6},{6,7},{7,4},{8,9},{9,10},{10,1... | collective-permute-start | bytes 3145736 | tf_op jit(solution)/shard_map/ppermute | solution.py:30
  211.7 5.2 %copy-start.9 = (bf16[128,4096]{1,0:T(8,128)(2,1)S(1)}, bf16[128,4096]{1,0:T(8,128)(2,1)}, u32[]{:S(2)}) copy-start(bf16[128,4096]{1,0:T(8,128)(2,1)} %gather_tokens.6.refs_2_) | copy-start | bytes 3145732
  211.7 2.1 collective-permute-start.21
  215.1 8.5 %collective-permute-start.22 = (bf16[2,128,512]{2,1,0:T(8,128)(2,1)S(1)}, bf16[2,128,512]{2,1,0:T(8,128)(2,1)}, u32[]{:S(2)}, u32[]{:S(2)}) collective-permute-start(bf16[2,128,512]{2,1,0:T(8,128)(2,1)S(1)} %fusion.3), channel_id=1, source_target_pairs={{0,8},{4,12},{8,0},{12,4},{16,24},{20,28},{24,16},{28,20},{1,9},{5... | collective-permute-start | bytes 786440 | tf_op jit(solution)/shard_map/ppermute | solution.py:25
  216.9 9.7 %copy-start.16 = (bf16[128,1024]{1,0:T(8,128)(2,1)S(1)}, bf16[128,1024]{1,0:T(8,128)(2,1)}, u32[]{:S(2)}) copy-start(bf16[128,1024]{1,0:T(8,128)(2,1)} %get-tuple-element.55.refs_0_) | copy-start | bytes 786436
  216.9 9.7 %copy-start.17 = (bf16[128,1024]{1,0:T(8,128)(2,1)S(1)}, bf16[128,1024]{1,0:T(8,128)(2,1)}, u32[]{:S(2)}) copy-start(bf16[128,1024]{1,0:T(8,128)(2,1)} %get-tuple-element.57.refs_0_) | copy-start | bytes 786436
  216.9 9.7 %copy-start.18 = (bf16[128,1024]{1,0:T(8,128)(2,1)S(1)}, bf16[128,1024]{1,0:T(8,128)(2,1)}, u32[]{:S(2)}) copy-start(bf16[128,1024]{1,0:T(8,128)(2,1)} %get-tuple-element.67.refs_0_) | copy-start | bytes 786436
  216.9 28.0 %collective-permute-start.24 = (bf16[128,4096]{1,0:T(8,128)(2,1)S(1)}, bf16[128,4096]{1,0:T(8,128)(2,1)}, u32[]{:S(2)}, u32[]{:S(2)}) collective-permute-start(bf16[128,4096]{1,0:T(8,128)(2,1)S(1)} %copy-done.9), channel_id=1, source_target_pairs={{0,1},{1,2},{2,3},{3,0},{4,5},{5,6},{6,7},{7,4},{8,9},{9,10},{10,1... | collective-permute-start | bytes 3145736 | tf_op jit(solution)/shard_map/ppermute | solution.py:30
  216.9 27.9 %all-to-all-start.4 = ((bf16[8,24,4096]{2,1,0:T(8,128)(2,1)}), bf16[8,24,4096]{2,1,0:T(8,128)(2,1)}, u32[]{:S(2)}, u32[]{:S(2)}) async-start(bf16[8,24,4096]{2,1,0:T(8,128)(2,1)} %expert_piece.7.refs_2_), calls=%async_computation.4 | async-start | bytes 3145728 | tf_op jit(solution)/shard_map/all_to_all | solution.py:421
  224.7 19.4 %collective-permute-start.23 = (bf16[1,128,512]{2,1,0:T(8,128)(2,1)S(1)}, bf16[1,128,512]{2,1,0:T(8,128)(2,1)S(1)}, u32[]{:S(2)}, u32[]{:S(2)}) collective-permute-start(bf16[1,128,512]{2,1,0:T(8,128)(2,1)S(1)} %fusion.5), channel_id=1, source_target_pairs={{0,16},{4,20},{8,24},{12,28},{16,0},{20,4},{24,8},{28,12},{1,17},{... | collective-permute-start | bytes 393224 | tf_op jit(solution)/shard_map/ppermute | solution.py:25
  (14 other events, 21.7 us)
